TPU v7x, 32 devices: a whole 2x2x4 slice. The times are simulated.
32 devices in a mesh: wide: 8 (over z, y), narrow: 4 (over x, core).
Axes of the slice: x: 2, y: 2, z: 4, core: 2. Of those that a mesh axis runs over, the one named last changes fastest.
Arguments:
- hidden: bfloat16 [8, 1024, 1024], P('wide', 'narrow'), may hold values from -6 to 6
- lengths: int32 [8], P('wide'), may hold values from 256 to 1024, as said below
- routes: int32 [8, 1024, 8], P('wide', 'narrow'), may hold values from 0 to 31, all different within a row; in each aligned block of 256 rows (0 to 255, 256 to 511, ..., all dimensions but the last counted through in order) at most 128 rows name the same one
- cotangent: bfloat16 [8, 1024, 1024], P('wide', 'narrow'), may hold values from -6 to 6
- attn_gain: float32 [1024], replicated, may hold values from 0.1 to 1.9
- w_query: bfloat16 [1024, 1024], P(None, 'narrow'), may hold values from -0.1875 to 0.1875
- w_key: bfloat16 [1024, 512], P(None, 'narrow'), may hold values from -0.1875 to 0.1875
- w_value: bfloat16 [1024, 512], P(None, 'narrow'), may hold values from -0.1875 to 0.1875
- w_out: bfloat16 [1024, 1024], P('narrow'), may hold values from -3 to 3
- moe_gain: float32 [1024], replicated, may hold values from 0.1 to 1.9
- w_router: bfloat16 [1024, 32], replicated, may hold values from -0.09375 to 0.09375
- w_gate_up: bfloat16 [32, 1024, 1024], P('wide'), may hold values from -0.1875 to 0.1875
- w_down: bfloat16 [32, 512, 1024], P('wide'), may hold values from -1 to 1
Outputs:
- out: bfloat16 [8, 1024, 1024], P('wide', 'narrow')
- grad_hidden: bfloat16 [8, 1024, 1024], P('wide', 'narrow')
- grad_attn_gain: float32 [1024], replicated
- grad_query: float32 [1024, 1024], P(None, 'narrow')
- grad_key: float32 [1024, 512], P(None, 'narrow')
- grad_value: float32 [1024, 512], P(None, 'narrow')
- grad_out: float32 [1024, 1024], P('narrow')
- grad_moe_gain: float32 [1024], replicated
- grad_router: float32 [1024, 32], replicated
- grad_gate_up: float32 [32, 1024, 1024], P('wide')
- grad_down: float32 [32, 512, 1024], P('wide')
Inputs may be any that keep to these rules, and one draw needn't show every extreme that they name: Row lengths; every row reaches 256 or more, one row has all 1024 positions and one exactly 256. A token's 8 routes name different experts. Within the 256 positions of one device (aligned blocks of a row) no expert is named by more than 128 tokens, a bound that some block reaches. Positions past a row's length carry routes too.
All inputs are finite; a program needn't handle non-finite values.
Results may differ from a plain program's by a relative error of at most 0.028.
Values may be sent and summed in bfloat16 or wider, within the bound.
A program may use at most 192 MiB of HBM per device.

v0:
```python
import jax
import jax.numpy as jnp
from jax import lax
from jax.sharding import PartitionSpec as P

HEADS = 16
KV_HEADS = 8
HEAD_DIM = 64


EPSILON = 1e-06
THETA = 10000.0
HIGHEST = lax.Precision.HIGHEST


def rope_tables(count, head_dim):
    half_dim = head_dim // 2
    inverse = THETA ** (-jnp.arange(half_dim, dtype=jnp.float32) * 2.0 / head_dim)
    angles = jnp.arange(count, dtype=jnp.float32)[:, None] * inverse[None, :]
    return (jnp.cos(angles), jnp.sin(angles))


def turn(values, cosine, sine_part, direction):
    half_dim = values.shape[-1] // 2
    shape_here = (cosine.shape[0],) + (1,) * (values.ndim - 2) + (half_dim,)
    cosine = cosine.reshape(shape_here)
    sine_part = direction * sine_part.reshape(shape_here)
    first = values[..., :half_dim]
    second = values[..., half_dim:]
    return jnp.concatenate(
        [first * cosine - second * sine_part, second * cosine + first * sine_part], axis=-1
    )


def norm_forward(values, gain):
    scaling = lax.rsqrt(jnp.mean(values * values, axis=-1, keepdims=True) + EPSILON)
    return (values * scaling * gain, scaling)


def norm_backward(values, scaling, gain, incoming):
    unit_values = values * scaling
    gain_grad = jnp.sum(incoming * unit_values, axis=0)
    inner = incoming * gain
    input_grad = scaling * (
        inner - unit_values * jnp.mean(inner * unit_values, axis=-1, keepdims=True)
    )
    return (input_grad, gain_grad)


def visible(start, block_rows, key_places, length_here):
    query_places = start + jnp.arange(block_rows, dtype=jnp.int32)
    return (key_places[None, :] <= query_places[:, None]) & (key_places[None, :] < length_here)


def attend_forward(queries, keys_low, values_low, length_here, scaling):
    key_places = jnp.arange(keys_low.shape[1], dtype=jnp.int32)
    block_rows = queries.shape[3]

    def one_block(inputs):
        query_block, start = inputs
        scores = (
            jnp.einsum("kgqd,ksd->kgqs", query_block, keys_low, preferred_element_type=jnp.float32)
            * scaling
        )
        scores = jnp.where(visible(start, block_rows, key_places, length_here), scores, -1e30)
        highest = jnp.max(scores, axis=-1, keepdims=True)
        weights = jnp.exp(scores - highest)
        totals = jnp.sum(weights, axis=-1, keepdims=True)
        chances = (weights / totals).astype(jnp.bfloat16)
        context = jnp.einsum(
            "kgqs,ksd->kgqd", chances, values_low, preferred_element_type=jnp.float32
        )
        return (context.astype(jnp.bfloat16), (highest + jnp.log(totals))[..., 0])

    starts = jnp.arange(queries.shape[0], dtype=jnp.int32) * block_rows
    return lax.map(one_block, (queries, starts))


def attend_backward(queries, keys_low, values_low, context_grad, log_sums, length_here, scaling):
    key_places = jnp.arange(keys_low.shape[1], dtype=jnp.int32)
    block_rows = queries.shape[3]

    def one_block(carry, inputs):
        key_grad, value_grad = carry
        query_block, grad_block, sum_block, start = inputs
        scores = (
            jnp.einsum("kgqd,ksd->kgqs", query_block, keys_low, preferred_element_type=jnp.float32)
            * scaling
        )
        allowed = visible(start, block_rows, key_places, length_here)
        scores = jnp.where(allowed, scores, -1e30)
        chances = jnp.where(allowed, jnp.exp(scores - sum_block[..., None]), 0.0)
        chance_grad = jnp.einsum(
            "kgqd,ksd->kgqs", grad_block, values_low, preferred_element_type=jnp.float32
        )
        inner = jnp.sum(chances * chance_grad, axis=-1, keepdims=True)
        score_grad = (chances * (chance_grad - inner)).astype(jnp.bfloat16)
        query_grad = (
            jnp.einsum("kgqs,ksd->kgqd", score_grad, keys_low, preferred_element_type=jnp.float32)
            * scaling
        )
        key_grad = (
            key_grad
            + jnp.einsum(
                "kgqs,kgqd->ksd", score_grad, query_block, preferred_element_type=jnp.float32
            )
            * scaling
        )
        value_grad = value_grad + jnp.einsum(
            "kgqs,kgqd->ksd",
            chances.astype(jnp.bfloat16),
            grad_block,
            preferred_element_type=jnp.float32,
        )
        return ((key_grad, value_grad), query_grad)

    starts = jnp.arange(queries.shape[0], dtype=jnp.int32) * block_rows
    zeros = jnp.zeros(keys_low.shape, jnp.float32)
    (key_grad, value_grad), query_grad = lax.scan(
        one_block, (zeros, zeros), (queries, context_grad, log_sums, starts)
    )
    return (query_grad, key_grad, value_grad)


def local(
    hidden,
    lengths,
    routes,
    cotangent,
    attn_gain,
    w_query,
    w_key,
    w_value,
    w_out,
    moe_gain,
    w_router,
    w_gate_up,
    w_down,
):
    rows_here = hidden.shape[1]
    width = hidden.shape[2]
    seq_len = rows_here * lax.axis_size("narrow")
    head_dim = HEAD_DIM
    group_size = HEADS // KV_HEADS
    kv_here = w_key.shape[1] // head_dim
    query_cols = kv_here * group_size * head_dim
    key_cols = kv_here * head_dim
    scaling = head_dim ** (-0.5)
    block_rows = min(512, seq_len)
    block_count = seq_len // block_rows
    length_here = lengths[0]
    offset = lax.axis_index("narrow") * rows_here
    local_places = offset + jnp.arange(rows_here, dtype=jnp.int32)
    valid = (local_places < length_here).astype(jnp.float32)[:, None]
    source = hidden[0].astype(jnp.float32)
    normed, scale_one = norm_forward(source, attn_gain)
    normed_low = normed.astype(jnp.bfloat16)
    whole = lax.all_gather(normed_low, "narrow", axis=0, tiled=True)
    w_qkv = jnp.concatenate([w_query, w_key, w_value], axis=1)
    projected = jnp.dot(whole, w_qkv, preferred_element_type=jnp.float32)
    cosine, sine_part = rope_tables(seq_len, head_dim)
    query_rot = turn(
        projected[:, :query_cols].reshape(seq_len, kv_here, group_size, head_dim),
        cosine,
        sine_part,
        1.0,
    )
    key_rot = turn(
        projected[:, query_cols : query_cols + key_cols].reshape(seq_len, kv_here, head_dim),
        cosine,
        sine_part,
        1.0,
    )
    queries = (
        query_rot.astype(jnp.bfloat16)
        .reshape(block_count, block_rows, kv_here, group_size, head_dim)
        .transpose(0, 2, 3, 1, 4)
    )
    keys_low = key_rot.astype(jnp.bfloat16).transpose(1, 0, 2)
    values_low = (
        projected[:, query_cols + key_cols :]
        .astype(jnp.bfloat16)
        .reshape(seq_len, kv_here, head_dim)
        .transpose(1, 0, 2)
    )
    context, log_sums = attend_forward(queries, keys_low, values_low, length_here, scaling)
    context_rows = context.transpose(0, 3, 1, 2, 4).reshape(seq_len, query_cols)
    piece = context_rows
    attn_part = lax.psum_scatter(
        jnp.dot(piece, w_out, preferred_element_type=jnp.float32).astype(jnp.bfloat16),
        "narrow",
        scatter_dimension=0,
        tiled=True,
    ).astype(jnp.float32)
    mixed = source + attn_part
    normed_two, scale_two = norm_forward(mixed, moe_gain)
    entry = normed_two.astype(jnp.bfloat16)
    logits = jnp.dot(entry, w_router, preferred_element_type=jnp.float32)
    route_here = routes[0]
    tokens_here, picks = route_here.shape
    expert_total = w_router.shape[1]
    capacity = 2 * tokens_here * picks // expert_total
    member = (
        route_here[:, :, None] == jnp.arange(expert_total, dtype=jnp.int32)[None, None, :]
    ).astype(jnp.int32)
    flat_member = member.reshape(tokens_here * picks, expert_total)
    earlier = jnp.cumsum(flat_member, axis=0) - flat_member
    slot_index = jnp.sum(earlier * flat_member, axis=1)
    places = route_here.reshape(-1) * capacity + slot_index
    member_float = member.astype(jnp.float32)
    chosen = jnp.einsum("tke,te->tk", member_float, logits, precision=HIGHEST)
    highest = jnp.max(chosen, axis=-1, keepdims=True)
    raised = jnp.exp(chosen - highest)
    shares = raised / jnp.sum(raised, axis=-1, keepdims=True)
    gates = shares * valid
    outgoing = (
        jnp.zeros((expert_total * capacity, width), jnp.bfloat16)
        .at[places]
        .set(jnp.repeat(entry, picks, axis=0))
    )
    received = lax.all_to_all(
        outgoing.reshape(expert_total, capacity, width),
        "wide",
        split_axis=0,
        concat_axis=1,
        tiled=True,
    )
    expert_pre = jnp.einsum("erd,edf->erf", received, w_gate_up, preferred_element_type=jnp.float32)
    ffe_width = w_down.shape[1]
    gate_part = expert_pre[..., :ffe_width]
    up_part = expert_pre[..., ffe_width:]
    sigmoid_gate = jax.nn.sigmoid(gate_part)
    swish = gate_part * sigmoid_gate
    act_low = (swish * up_part).astype(jnp.bfloat16)
    expert_result = jnp.einsum(
        "erf,efd->erd", act_low, w_down, preferred_element_type=jnp.float32
    ).astype(jnp.bfloat16)
    returned = lax.all_to_all(expert_result, "wide", split_axis=1, concat_axis=0, tiled=True)
    picked = returned.reshape(expert_total * capacity, width)[places].reshape(
        tokens_here, picks, width
    )
    expert_sum = jnp.einsum("tk,tkd->td", gates, picked, precision=HIGHEST)
    output_rows = (valid * (mixed + expert_sum)).astype(jnp.bfloat16)
    grad_rows_here = cotangent[0].astype(jnp.float32) * valid
    slot_grad = (gates[:, :, None] * grad_rows_here[:, None, :]).astype(jnp.bfloat16)
    grad_outgoing = (
        jnp.zeros((expert_total * capacity, width), jnp.bfloat16)
        .at[places]
        .set(slot_grad.reshape(tokens_here * picks, width))
    )
    grad_received = lax.all_to_all(
        grad_outgoing.reshape(expert_total, capacity, width),
        "wide",
        split_axis=0,
        concat_axis=1,
        tiled=True,
    )
    act_grad = jnp.einsum("erd,efd->erf", grad_received, w_down, preferred_element_type=jnp.float32)
    down_grad = jnp.einsum(
        "erf,erd->efd", act_low, grad_received, preferred_element_type=jnp.float32
    )
    gate_grad = act_grad * up_part * sigmoid_gate * (1.0 + gate_part * (1.0 - sigmoid_gate))
    pre_grad = jnp.concatenate([gate_grad, act_grad * swish], axis=-1).astype(jnp.bfloat16)
    gate_up_grad = jnp.einsum(
        "erd,erf->edf", received, pre_grad, preferred_element_type=jnp.float32
    )
    entry_back = jnp.einsum(
        "erf,edf->erd", pre_grad, w_gate_up, preferred_element_type=jnp.float32
    ).astype(jnp.bfloat16)
    entry_home = lax.all_to_all(entry_back, "wide", split_axis=1, concat_axis=0, tiled=True)
    entry_rows = entry_home.reshape(expert_total * capacity, width)[places].reshape(
        tokens_here, picks, width
    )
    entry_grad = jnp.sum(entry_rows, axis=1, dtype=jnp.float32)
    pick_grad = jnp.einsum("td,tkd->tk", grad_rows_here, picked, precision=HIGHEST) * valid
    chosen_grad = shares * (pick_grad - jnp.sum(shares * pick_grad, axis=-1, keepdims=True))
    logit_grad = jnp.einsum("tk,tke->te", chosen_grad, member_float, precision=HIGHEST)
    router_grad = lax.dot_general(
        entry.astype(jnp.float32), logit_grad, (((0,), (0,)), ((), ())), precision=HIGHEST
    )
    entry_grad = entry_grad + lax.dot_general(
        logit_grad, w_router.astype(jnp.float32), (((1,), (1,)), ((), ())), precision=HIGHEST
    )
    mixed_from_norm, gain_two_grad = norm_backward(mixed, scale_two, moe_gain, entry_grad)
    mixed_grad = grad_rows_here + mixed_from_norm
    attn_grad_low = mixed_grad.astype(jnp.bfloat16)
    grad_whole = lax.all_gather(attn_grad_low, "narrow", axis=0, tiled=True)
    context_grad = lax.dot_general(
        grad_whole, w_out, (((1,), (1,)), ((), ())), preferred_element_type=jnp.float32
    ).astype(jnp.bfloat16)
    out_grad = lax.dot_general(
        context_rows, grad_whole, (((0,), (0,)), ((), ())), preferred_element_type=jnp.float32
    )
    context_blocks = context_grad.reshape(
        block_count, block_rows, kv_here, group_size, head_dim
    ).transpose(0, 2, 3, 1, 4)
    query_grad, key_grad, value_grad = attend_backward(
        queries, keys_low, values_low, context_blocks, log_sums, length_here, scaling
    )
    query_rows = turn(
        query_grad.transpose(0, 3, 1, 2, 4).reshape(seq_len, kv_here, group_size, head_dim),
        cosine,
        sine_part,
        -1.0,
    )
    key_rows = turn(key_grad.transpose(1, 0, 2), cosine, sine_part, -1.0)
    value_rows = value_grad.transpose(1, 0, 2)
    qkv_grad = jnp.concatenate(
        [
            query_rows.reshape(seq_len, query_cols),
            key_rows.reshape(seq_len, key_cols),
            value_rows.reshape(seq_len, key_cols),
        ],
        axis=1,
    ).astype(jnp.bfloat16)
    qkv_weight_grad = lax.dot_general(
        whole, qkv_grad, (((0,), (0,)), ((), ())), preferred_element_type=jnp.float32
    )
    piece = qkv_grad
    normed_grad = lax.psum_scatter(
        lax.dot_general(
            piece, w_qkv, (((1,), (1,)), ((), ())), preferred_element_type=jnp.float32
        ).astype(jnp.bfloat16),
        "narrow",
        scatter_dimension=0,
        tiled=True,
    ).astype(jnp.float32)
    source_from_norm, gain_one_grad = norm_backward(source, scale_one, attn_gain, normed_grad)
    grad_input = (mixed_grad + source_from_norm).astype(jnp.bfloat16)
    gate_up_grad, down_grad, router_grad, gain_one_grad, gain_two_grad = (
        lax.psum(gate_up_grad.astype(jnp.bfloat16), "narrow").astype(jnp.float32),
        lax.psum(down_grad.astype(jnp.bfloat16), "narrow").astype(jnp.float32),
        lax.psum(router_grad.astype(jnp.bfloat16), "narrow").astype(jnp.float32),
        lax.psum(gain_one_grad.astype(jnp.bfloat16), "narrow").astype(jnp.float32),
        lax.psum(gain_two_grad.astype(jnp.bfloat16), "narrow").astype(jnp.float32),
    )
    qkv_weight_grad, out_grad, router_grad, gain_one_grad, gain_two_grad = (
        lax.psum(qkv_weight_grad.astype(jnp.bfloat16), "wide").astype(jnp.float32),
        lax.psum(out_grad.astype(jnp.bfloat16), "wide").astype(jnp.float32),
        lax.psum(router_grad.astype(jnp.bfloat16), "wide").astype(jnp.float32),
        lax.psum(gain_one_grad.astype(jnp.bfloat16), "wide").astype(jnp.float32),
        lax.psum(gain_two_grad.astype(jnp.bfloat16), "wide").astype(jnp.float32),
    )
    query_weight_grad = qkv_weight_grad[:, :query_cols]
    key_weight_grad = qkv_weight_grad[:, query_cols : query_cols + key_cols]
    value_weight_grad = qkv_weight_grad[:, query_cols + key_cols :]
    return (
        output_rows[None],
        grad_input[None],
        gain_one_grad,
        query_weight_grad,
        key_weight_grad,
        value_weight_grad,
        out_grad,
        gain_two_grad,
        router_grad,
        gate_up_grad,
        down_grad,
    )


def solution(mesh):
    in_specs = (
        P("wide", "narrow", None),
        P("wide"),
        P("wide", "narrow", None),
        P("wide", "narrow", None),
        P(),
        P(None, "narrow"),
        P(None, "narrow"),
        P(None, "narrow"),
        P("narrow", None),
        P(),
        P(),
        P("wide", None, None),
        P("wide", None, None),
    )
    out_specs = (
        P("wide", "narrow", None),
        P("wide", "narrow", None),
        P(),
        P(None, "narrow"),
        P(None, "narrow"),
        P(None, "narrow"),
        P("narrow", None),
        P(),
        P(),
        P("wide", None, None),
        P("wide", None, None),
    )
    return jax.shard_map(local, mesh=mesh, in_specs=in_specs, out_specs=out_specs, check_vma=False)
```

profile of v0, /device:TPU:0, one launch (start us, length us, event | category | flops | bytes accessed | tf_op | source)
XLA Modules:
  0.0 1381.2 jit_solution(18058803103629947972)
XLA Ops:
  17.7 18.9 %all-gather.3.cloned.1.call-done = bf16[1024,1024]{1,0:T(8,128)(2,1)} async-done(((bf16[256,1024]{1,0:T(8,128)(2,1)}), bf16[1024,1024]{1,0:T(8,128)(2,1)}) %all-gather.3.cloned.1.call-update) | async-done | bytes 2097168 | tf_op jit(solution)/shard_map/all_gather | solution.py:158
  43.5 22.1 %while.30 = (s32[]{:T(128)}, bf16[2,2,2,512,64]{3,4,2,1,0:T(8,128)(2,1)S(1)}, f32[2,2,2,512]{3,2,1,0:T(2,128)S(1)}, s32[2]{0:T(128)S(1)}, s32[]{:T(128)}, /*inde...) while((s32[]{:T(128)}, ...), condition=%wide.region_4.5_spmd.clone.clone, body=%wide.region_1.4_spmd.clone.clone.sunk | while | flops 563215872 | bytes 28383364 | solution.py:76
  70.6 9.1 reduce-window.6
  81.8 19.2 %reduce-scatter.3.cloned.1.call-done = bf16[256,1024]{1,0:T(8,128)(2,1)} async-done(((bf16[1024,1024]{1,0:T(8,128)(2,1)}), bf16[256,1024]{1,0:T(8,128)(2,1)}) %reduce-scatter.3.cloned.1.call-update) | async-done | bytes 524304 | tf_op jit(solution)/shard_map/reduce_scatter | solution.py:189
  106.7 15.8 %scatter_custom_fusion.1 = bf16[4096,1024]{1,0:T(8,128)(2,1)} fusion(s32[2048]{0:T(1024)S(1)} %bitcast.333, f32[256,1024]{1,0:T(8,128)S(1)} %get-tuple-element.350, f32[2048]{0:T(1024)S(1)} %mul.537, bf16[]{:T(256)} %constant.44.clone.1), kind=kCustom, calls=%fused_computation.74 | custom fusion | flops 4194304 | bytes 9445378 | tf_op jit(solution)/shard_map/scatter | solution.py:249
  128.0 15.1 %scatter_custom_fusion = bf16[4096,1024]{1,0:T(8,128)(2,1)} fusion(s32[2048]{0:T(1024)S(1)} %bitcast.334, bf16[]{:T(256)} %constant.44.clone.1, bf16[256,1024]{1,0:T(8,128)(2,1)S(1)} %multiply_convert_fusion.4), kind=kCustom, calls=%fused_computation.79 | custom fusion | bytes 8912898 | tf_op jit(solution)/shard_map/scatter | solution.py:219
  143.2 168.0 %all-to-all-done.2 = bf16[32,128,1024]{2,1,0:T(8,128)(2,1)} async-done(((bf16[32,128,1024]{2,1,0:T(8,128)(2,1)}), bf16[32,128,1024]{2,1,0:T(8,128)(2,1)}, u32[]{:S(2)}, u32[]{:S(2)}) %all-to-all-start.2) | async-done | bytes 8388640 | tf_op jit(solution)/shard_map/all_to_all | solution.py:251
  316.2 8.2 copy.67
  324.5 174.0 %all-to-all-done = bf16[32,128,1024]{2,1,0:T(8,128)(2,1)} async-done(((bf16[32,128,1024]{2,1,0:T(8,128)(2,1)}), bf16[32,128,1024]{2,1,0:T(8,128)(2,1)}, u32[]{:S(2)}, u32[]{:S(2)}) %all-to-all-start) | async-done | bytes 8388640 | tf_op jit(solution)/shard_map/all_to_all | solution.py:221
  498.4 8.4 copy.62
  506.8 17.2 %fusion.106 = f32[4,1024,1024]{1,2,0:T(8,128)} fusion(bf16[4,1024,1024]{2,1,0:T(8,128)(2,1)} %bitcast.299, bf16[4,1024,1024]{2,1,0:T(8,128)(2,1)} %param.28), kind=kOutput, calls=%fused_computation.186 | convolution fusion | flops 8589934592 | bytes 33554432 | tf_op jit(solution)/shard_map/erd,edf->erf/dot_general | solution.py:228
  524.0 16.5 %multiply_convert_fusion.2 = (bf16[4,1024,512]{1,2,0:T(8,128)(2,1)}, bf16[4,1024,512]{1,2,0:T(8,128)(2,1)}, bf16[4,1024,512]{1,2,0:T(8,128)(2,1)}) fusion(f32[4,1024,1024]{1,2,0:T(8,128)} %fusion.106, bf16[4,1024,1024]{2,1,0:T(8,128)(2,1)} %bitcast.297, bf16[4,512,1024]{2,1,0:T(8,128)(2,1)} %param.29), kind=kOutput, calls=%fused_computation.67 | convolution fusion | flops 4326424576 | bytes 41943040 | tf_op jit(solution)/shard_map/erd,efd->erf/dot_general | solution.py:258
  540.5 16.6 %convolution_convert_fusion.1 = bf16[4,1024,1024]{2,1,0:T(8,128)(2,1)} fusion(bf16[4,1024,1024]{2,1,0:T(8,128)(2,1)} %param.28, bf16[4,1024,512]{1,2,0:T(8,128)(2,1)} %get-tuple-element.335, bf16[4,1024,512]{1,2,0:T(8,128)(2,1)} %get-tuple-element.334), kind=kOutput, calls=%fused_computation.72 | convolution fusion | flops 8610906112 | bytes 25165824 | tf_op jit(solution)/shard_map/erf,edf->erd/dot_general | solution.py:267
  557.0 12.2 copy.69
  574.5 8.0 convolution_convert_fusion.2
  582.5 22.8 %copy.65 = bf16[4,1024,1024]{2,0,1:T(4,128)(2,1)} copy(bf16[4,1024,1024]{2,1,0:T(8,128)(2,1)S(1)} %convolution_convert_fusion.2) | data formatting | bytes 16777216 | tf_op jit(solution)/shard_map/convert_element_type | solution.py:237
  605.3 151.1 %all-to-all-done.3 = bf16[4,1024,1024]{2,0,1:T(4,128)(2,1)} async-done(((bf16[4,1024,1024]{2,0,1:T(4,128)(2,1)}), bf16[4,1024,1024]{2,0,1:T(4,128)(2,1)}, u32[]{:S(2)}, u32[]{:S(2)}) %all-to-all-start.3) | async-done | bytes 8388640 | tf_op jit(solution)/shard_map/all_to_all | solution.py:270
  761.5 10.0 copy.70
  771.4 15.9 %gather_fusion.1 = bf16[2048,1024]{1,0:T(8,128)(2,1)} fusion(bf16[4096,1024]{1,0:T(8,128)(2,1)} %bitcast.293, s32[2048]{0:T(1024)S(1)} %broadcast_clamp_fusion), kind=kCustom, calls=%fused_computation.1 | custom fusion | bytes 8396800 | tf_op jit(solution)/shard_map/gather | solution.py:271
  792.8 150.8 %all-to-all-done.1 = bf16[4,1024,1024]{2,0,1:T(4,128)(2,1)} async-done(((bf16[4,1024,1024]{2,0,1:T(4,128)(2,1)}), bf16[4,1024,1024]{2,0,1:T(4,128)(2,1)}, u32[]{:S(2)}, u32[]{:S(2)}) %all-to-all-start.1) | async-done | bytes 8388640 | tf_op jit(solution)/shard_map/all_to_all | solution.py:238
  943.6 10.0 copy.66
  953.6 15.7 %gather_fusion = bf16[2048,1024]{1,0:T(8,128)(2,1)} fusion(bf16[4096,1024]{1,0:T(8,128)(2,1)} %bitcast.292, s32[2048]{0:T(1024)S(1)} %broadcast_clamp_fusion), kind=kCustom, calls=%fused_computation | custom fusion | bytes 8396800 | tf_op jit(solution)/shard_map/gather | solution.py:239
  969.4 10.0 fusion.52
  985.9 11.2 convolution_convert_fusion.3
  997.2 16.5 %convolution_convert_fusion = bf16[4,1024,1024]{2,1,0:T(8,128)(2,1)} fusion(bf16[4,1024,1024]{2,1,0:T(8,128)(2,1)} %bitcast.300, bf16[4,1024,512]{1,2,0:T(8,128)(2,1)} %get-tuple-element.335, bf16[4,1024,512]{1,2,0:T(8,128)(2,1)} %get-tuple-element.334), kind=kOutput, calls=%fused_computation.71 | convolution fusion | flops 8610906112 | bytes 25165824 | tf_op jit(solution)/shard_map/erd,erf->edf/dot_general | solution.py:264
  1018.3 33.4 %while.31 = (s32[]{:T(128)}, f32[2,1024,64]{1,2,0:T(8,128)S(1)}, f32[2,1024,64]{1,2,0:T(8,128)S(1)}, f32[2,2,2,512,64]{3,4,2,1,0:T(8,128)}, s32[2]{0:T(128)S(1)}...) while((s32[]{:T(128)}, f32[2,1024,64]{1,2,0:T(8,128)S(1)}, ...), condition=%wide.region_19.20_spmd.clone.clone, body=%wide.region_17.19_spmd.clone.clone.sunk | while | flops 1364983296 | bytes 76855528 | solution.py:119
  1064.5 171.0 %all-reduce.9.cloned.1.call-done = (bf16[1024,32]{0,1:T(8,128)(2,1)}, bf16[4,1024,1024]{2,1,0:T(8,128)(2,1)}, bf16[4,512,1024]{2,1,0:T(8,128)(2,1)}) async-done(((bf16[1024,32]{0,1:T(8,128)(2,1)}, bf16[4,1024,1024]{2,1,0:T(8,128)(2,1)}, bf16[4,512,1024]{2,1,0:T(8,128)(2,1)}), (bf16[1024,32]{0,1:T(8,128)(2,1)}, bf16[4,1024,1024]{2,1,0:T(8,128)(2,1)}, ...) | async-done | bytes 12648464 | tf_op jit(solution)/shard_map/psum | solution.py:333
  1242.2 7.0 convert_element_type.191
  1249.3 11.9 convert_element_type.189
  1261.2 8.5 reduce-scatter.5.cloned.1.call-done
  1277.0 22.6 %all-reduce = (bf16[1024]{0:T(1024)(128)(2,1)S(1)}, bf16[1024]{0:T(1024)(128)(2,1)S(1)}) all-reduce(bf16[1024]{0:T(1024)(128)(2,1)S(1)} %get-tuple-element.325, bf16[1024]{0:T(1024)(128)(2,1)S(1)} %get-tuple-element.326), channel_id=1, replica_groups=mesh['wide'=8,'narrow'=4] {'wide'}, use_global_device_ids=true, to_apply=%region_24.25 | all-reduce | flops 2048 | bytes 8192 | tf_op jit(solution)/shard_map/psum | solution.py:341
  1304.1 62.3 %all-reduce.7.cloned.1.call-done = (bf16[1024,512]{1,0:T(8,128)(2,1)}, bf16[256,1024]{1,0:T(8,128)(2,1)}, bf16[1024,32]{0,1:T(8,128)(2,1)}) async-done(((bf16[1024,512]{1,0:T(8,128)(2,1)}, bf16[256,1024]{1,0:T(8,128)(2,1)}, bf16[1024,32]{0,1:T(8,128)(2,1)}), (bf16[1024,512]{1,0:T(8,128)(2,1)}, bf16[256,1024]{1,0:T(8,128)(2,1)}, bf16[1024,32]{0,1:T(8,128)(2,1)})) %all-reduce.7.cloned.1.call-update) | async-done | bytes 1638416 | tf_op jit(solution)/shard_map/psum | solution.py:338
  (251 shorter events, 160.5 us)
Async XLA Ops:
  7.2 59.9 %copy-start = (bf16[256,1024]{1,0:T(8,128)(2,1)S(1)}, bf16[256,1024]{1,0:T(8,128)(2,1)}, u32[]{:S(2)}) copy-start(bf16[256,1024]{1,0:T(8,128)(2,1)} %param.25) | copy-start | bytes 1572868
  7.2 29.4 %all-gather.3.cloned.1.call-start = ((), (), s32[]{:S(2)}) async-start(), calls=%async_computation.6 | async-start | bytes 2621440 | tf_op jit(solution)/shard_map/all_gather | solution.py:158
  11.2 89.8 %reduce-scatter.3.cloned.1.call-start = ((), (), s32[]{:S(2)}) async-start(), calls=%async_computation.7 | async-start | bytes 2621440 | tf_op jit(solution)/shard_map/reduce_scatter | solution.py:189
  43.5 26.4 %copy-start.31 = (s32[1,256,8]{1,2,0:T(8,128)S(1)}, s32[1,256,8]{1,2,0:T(8,128)}, u32[]{:S(2)}) copy-start(s32[1,256,8]{1,2,0:T(8,128)} %param.19) | copy-start | bytes 24580
  65.6 40.1 %copy-start.29 = (f32[2,2,2,512]{3,2,1,0:T(2,128)}, f32[2,2,2,512]{3,2,1,0:T(2,128)S(1)}, u32[]{:S(2)}) copy-start(f32[2,2,2,512]{3,2,1,0:T(2,128)S(1)} %get-tuple-element.514) | copy-start | bytes 49156
  65.6 40.1 %copy-start.51 = (s32[2]{0:T(128)}, s32[2]{0:T(128)S(1)}, u32[]{:S(2)}) copy-start(s32[2]{0:T(128)S(1)} %get-tuple-element.597) | copy-start | bytes 28
  65.6 35.3 %copy-start.1 = (bf16[1,256,1024]{2,1,0:T(8,128)(2,1)S(1)}, bf16[1,256,1024]{2,1,0:T(8,128)(2,1)}, u32[]{:S(2)}) copy-start(bf16[1,256,1024]{2,1,0:T(8,128)(2,1)} %param.17) | copy-start | bytes 1572868
  65.6 36.6 %copy-start.32 = (f32[1024]{0:T(1024)S(1)}, f32[1024]{0:T(1024)}, u32[]{:S(2)}) copy-start(f32[1024]{0:T(1024)} %param.26) | copy-start | bytes 12292
  65.7 37.8 %copy-start.25 = (bf16[1024,32]{0,1:T(8,128)(2,1)S(1)}, bf16[1024,32]{0,1:T(8,128)(2,1)}, u32[]{:S(2)}) copy-start(bf16[1024,32]{0,1:T(8,128)(2,1)} %param.27) | copy-start | bytes 196612
  70.6 51.9 %copy-start.27 = (s32[256,8]{1,0:T(8,128)}, s32[256,8]{1,0:T(8,128)S(1)}, u32[]{:S(2)}) copy-start(s32[256,8]{1,0:T(8,128)S(1)} %copy.56) | copy-start | bytes 24580
  80.3 42.2 %copy-start.35 = (f32[256]{0:T(256)}, f32[256]{0:T(256)S(1)}, u32[]{:S(2)}) copy-start(f32[256]{0:T(256)S(1)} %compare_convert_fusion) | copy-start | bytes 3076
  122.5 188.7 %all-to-all-start.2 = ((bf16[32,128,1024]{2,1,0:T(8,128)(2,1)}), bf16[32,128,1024]{2,1,0:T(8,128)(2,1)}, u32[]{:S(2)}, u32[]{:S(2)}) async-start(bf16[32,128,1024]{2,1,0:T(8,128)(2,1)} %bitcast.296), calls=%async_computation.3 | async-start | bytes 16777216 | tf_op jit(solution)/shard_map/all_to_all | solution.py:251
  311.2 187.2 %all-to-all-start = ((bf16[32,128,1024]{2,1,0:T(8,128)(2,1)}), bf16[32,128,1024]{2,1,0:T(8,128)(2,1)}, u32[]{:S(2)}, u32[]{:S(2)}) async-start(bf16[32,128,1024]{2,1,0:T(8,128)(2,1)} %bitcast.295), calls=%async_computation.1 | async-start | bytes 16777216 | tf_op jit(solution)/shard_map/all_to_all | solution.py:221
  569.3 187.2 %all-to-all-start.3 = ((bf16[4,1024,1024]{2,0,1:T(4,128)(2,1)}), bf16[4,1024,1024]{2,0,1:T(4,128)(2,1)}, u32[]{:S(2)}, u32[]{:S(2)}) async-start(bf16[4,1024,1024]{2,0,1:T(4,128)(2,1)} %copy.69), calls=%async_computation.4 | async-start | bytes 16777216 | tf_op jit(solution)/shard_map/all_to_all | solution.py:270
  756.4 187.2 %all-to-all-start.1 = ((bf16[4,1024,1024]{2,0,1:T(4,128)(2,1)}), bf16[4,1024,1024]{2,0,1:T(4,128)(2,1)}, u32[]{:S(2)}, u32[]{:S(2)}) async-start(bf16[4,1024,1024]{2,0,1:T(4,128)(2,1)} %copy.65), calls=%async_computation.2 | async-start | bytes 16777216 | tf_op jit(solution)/shard_map/all_to_all | solution.py:238
  761.4 253.8 %all-gather.5.cloned.1.call-start = ((), (), s32[]{:S(2)}) async-start(), calls=%async_computation.8 | async-start | bytes 2621440 | tf_op jit(solution)/shard_map/all_gather | solution.py:287
  953.6 25.8 %copy-start.36 = (f32[256]{0:T(256)S(1)}, f32[256]{0:T(256)}, u32[]{:S(2)}) copy-start(f32[256]{0:T(256)} %copy-done.35) | copy-start | bytes 3076
  953.6 25.8 %copy-start.43 = (f32[256]{0:T(256)S(1)}, f32[256]{0:T(256)}, u32[]{:S(2)}) copy-start(f32[256]{0:T(256)} %copy-done.42) | copy-start | bytes 3076
  953.6 25.8 %copy-start.45 = (f32[256]{0:T(256)S(1)}, f32[256]{0:T(256)}, u32[]{:S(2)}) copy-start(f32[256]{0:T(256)} %copy-done.44) | copy-start | bytes 3076
  985.6 249.9 %all-reduce.9.cloned.1.call-start = ((), (), s32[]{:S(2)}) async-start(), calls=%async_computation.11 | async-start | bytes 25296896 | tf_op jit(solution)/shard_map/psum | solution.py:333
  1014.7 254.9 %reduce-scatter.5.cloned.1.call-start = ((), (), s32[]{:S(2)}) async-start(), calls=%async_computation.9 | async-start | bytes 2621440 | tf_op jit(solution)/shard_map/reduce_scatter | solution.py:320
  1018.2 34.8 %copy-start.14 = (f32[1024,32]{0,1:T(8,128)S(1)}, f32[1024,32]{0,1:T(8,128)}, u32[]{:S(2)}) copy-start(f32[1024,32]{0,1:T(8,128)} %copy-done.13) | copy-start | bytes 393220
  1018.2 34.8 %copy-start.19 = (f32[1024,32]{0,1:T(8,128)S(1)}, f32[1024,32]{0,1:T(8,128)}, u32[]{:S(2)}) copy-start(f32[1024,32]{0,1:T(8,128)} %get-tuple-element.351) | copy-start | bytes 393220
  1057.3 178.2 %copy-start.21 = (f32[256,8]{1,0:T(8,128)S(1)}, f32[256,8]{1,0:T(8,128)}, u32[]{:S(2)}) copy-start(f32[256,8]{1,0:T(8,128)} %copy-done.20) | copy-start | bytes 24580
  1057.3 309.0 %all-reduce.7.cloned.1.call-start = ((), (), s32[]{:S(2)}) async-start(), calls=%async_computation.10 | async-start | bytes 3276800 | tf_op jit(solution)/shard_map/psum | solution.py:338
  1249.2 51.5 %copy-start.5 = (bf16[256,1024]{1,0:T(8,128)(2,1)S(1)}, bf16[256,1024]{1,0:T(8,128)(2,1)}, u32[]{:S(2)}) copy-start(bf16[256,1024]{1,0:T(8,128)(2,1)} %reduce-scatter.3.cloned.1.call-done) | copy-start | bytes 1572868
  1249.2 51.5 %copy-start.7 = (f32[256,1024]{1,0:T(8,128)S(1)}, f32[256,1024]{1,0:T(8,128)}, u32[]{:S(2)}) copy-start(f32[256,1024]{1,0:T(8,128)} %copy-done.6) | copy-start | bytes 3145732
  1249.2 51.5 %copy-start.12 = (bf16[1,256,1024]{2,1,0:T(8,128)(2,1)S(1)}, bf16[1,256,1024]{2,1,0:T(8,128)(2,1)}, u32[]{:S(2)}) copy-start(bf16[1,256,1024]{2,1,0:T(8,128)(2,1)} %param.20) | copy-start | bytes 1572868
  1249.3 51.5 %copy-start.34 = (f32[1024]{0:T(1024)S(1)}, f32[1024]{0:T(1024)}, u32[]{:S(2)}) copy-start(f32[1024]{0:T(1024)} %param.26) | copy-start | bytes 12292
  1249.3 51.5 %copy-start.37 = (f32[256]{0:T(256)S(1)}, f32[256]{0:T(256)}, u32[]{:S(2)}) copy-start(f32[256]{0:T(256)} %copy-done.35) | copy-start | bytes 3076
  1249.3 51.5 %copy-start.41 = (f32[256]{0:T(256)S(1)}, f32[256]{0:T(256)}, u32[]{:S(2)}) copy-start(f32[256]{0:T(256)} %copy-done.39) | copy-start | bytes 3076
  1249.3 51.5 %copy-start.49 = (f32[256]{0:T(256)S(1)}, f32[256]{0:T(256)}, u32[]{:S(2)}) copy-start(f32[256]{0:T(256)} %copy-done.48) | copy-start | bytes 3076
  (33 other events, 384.5 us)
Sparse Core Ops, SparseCore 0:
  11.3 25.2 all-gather.2
  69.3 31.5 reduce-scatter.2
  985.8 20.8 all-gather.4
  1014.9 220.6 all-reduce.8
  1238.1 31.5 reduce-scatter.4
  1274.0 92.3 all-reduce.6
where the time goes:
time: 1390 us; the launch traced here: 1380 us
  waiting for transfers between devices  924 us (66%)
  matrix products  165 us (12%)
  local copies, waits for them, and re-layouts  141 us (10%)
  other arithmetic  85 us (6%)
  blocking collectives  28.3 us (2%)
  starting transfers between devices  21.8 us (2%)
  between operations  15.9 us (1%)
    all_to_all x1, waiting for transfers between devices, local(): lax.all_to_all(outgoing.reshape(expert_total, capacity, width), 'wide', s...  174 us
    psum x1, waiting for transfers between devices, local(): lax.psum(router_grad.astype(jnp.bfloat16), 'narrow').astype(jnp.float32)  171 us
    all_to_all x1, waiting for transfers between devices, local(): lax.all_to_all(grad_outgoing.reshape(expert_total, capacity, width), 'wid...  168 us
    all_to_all x1, waiting for transfers between devices, local(): lax.all_to_all(entry_back, 'wide', split_axis=1, concat_axis=0, tiled=True)  151 us
    all_to_all x1, waiting for transfers between devices, local(): lax.all_to_all(expert_result, 'wide', split_axis=1, concat_axis=0, tiled=...  151 us
    psum x1, waiting for transfers between devices, local(): lax.psum(qkv_weight_grad.astype(jnp.bfloat16), 'wide').astype(jnp.float32)  62.3 us
  transfers between devices with their start and end apart: 10, of which 9 were waited for; matrix products, arithmetic and copies ran while one was open for 15% of the time, Pallas kernels for 0%

commit v1 on v0

--- a/solution.py
+++ b/solution.py
@@ -1,13 +1,16 @@
+import functools
 import jax
 import jax.numpy as jnp
 from jax import lax
+from jax.experimental import pallas as pl
+from jax.experimental.pallas import tpu as pltpu
 from jax.sharding import PartitionSpec as P
 
 HEADS = 16
 KV_HEADS = 8
 HEAD_DIM = 64
-
-
+BF = jnp.bfloat16
+F32 = jnp.float32
 EPSILON = 1e-06
 THETA = 10000.0
 HIGHEST = lax.Precision.HIGHEST
@@ -122,6 +125,372 @@
     return (query_grad, key_grad, value_grad)
 
 
+MESH = pl.DeviceIdType.MESH
+
+def ring_place(index, count):
+    half = index // 2
+    odd = index % 2
+    return (1 - odd) * half + odd * (count - 1 - half)
+
+def ring_index(place, count):
+    odd = place // (count // 2)
+    half = (1 - odd) * place + odd * (count - 1 - place)
+    return 2 * half + odd
+
+def ring_greet(nxt, prv):
+    barrier = pltpu.get_barrier_semaphore()
+    for peer in (nxt, prv):
+        pl.semaphore_signal(barrier, inc=1, device_id={"wide": peer}, device_id_type=MESH)
+    pl.semaphore_wait(barrier, 2)
+
+def ring_gather(block, count, cid):
+    rows, cols = block.shape
+    hops = count // 2
+    part = rows // 2
+
+    def kernel(x_ref, o_ref, own_sem, send_sem, recv_sem):
+        me = lax.axis_index("wide")
+        place = ring_place(me, count)
+        at = lambda shift: ring_index((place + shift + 2 * count) % count, count)
+        peers = (at(1), at(-1))
+        ring_greet(*peers)
+        own = pltpu.make_async_copy(x_ref, o_ref.at[me], own_sem)
+        own.start()
+        live = lambda way, hop, k: hop < hops - 1 or k == way
+
+        def copy(way, hop, k, source):
+            sign = 1 if way == 0 else -1
+            index = at(-sign * hop)
+            span = pl.ds(k * part, part)
+            return pltpu.make_async_remote_copy(
+                src_ref=x_ref.at[span] if hop == 0 else o_ref.at[index, span],
+                dst_ref=o_ref.at[index, span],
+                send_sem=send_sem.at[way, hop, k],
+                recv_sem=recv_sem.at[way, hop, k],
+                device_id={"wide": peers[way]},
+                device_id_type=MESH,
+            )
+
+        def arrival(way, hop, k):
+            sign = 1 if way == 0 else -1
+            index = at(-sign * (hop + 1))
+            span = pl.ds(k * part, part)
+            return pltpu.make_async_remote_copy(
+                src_ref=o_ref.at[index, span],
+                dst_ref=o_ref.at[index, span],
+                send_sem=send_sem.at[way, hop, k],
+                recv_sem=recv_sem.at[way, hop, k],
+                device_id={"wide": peers[way]},
+                device_id_type=MESH,
+            )
+
+        order = [(h, k, w) for h in range(hops) for k in range(2) for w in range(2) if live(w, h, k)]
+        for hop, k, way in order:
+            if hop > 0:
+                arrival(way, hop - 1, k).wait_recv()
+            copy(way, hop, k, None).start()
+        for hop, k, way in order:
+            if not (hop + 1 < hops and live(way, hop + 1, k)):
+                arrival(way, hop, k).wait_recv()
+        for hop, k, way in order:
+            copy(way, hop, k, None).wait_send()
+        own.wait()
+
+    return pl.pallas_call(
+        kernel,
+        out_shape=jax.ShapeDtypeStruct((count, rows, cols), block.dtype),
+        in_specs=[pl.BlockSpec(memory_space=pl.ANY)],
+        out_specs=pl.BlockSpec(memory_space=pl.ANY),
+        scratch_shapes=[
+            pltpu.SemaphoreType.DMA,
+            pltpu.SemaphoreType.DMA((2, hops, 2)),
+            pltpu.SemaphoreType.DMA((2, hops, 2)),
+        ],
+        compiler_params=pltpu.CompilerParams(collective_id=cid, has_side_effects=True),
+    )(block)
+
+def ring_scatter(parts, cid):
+    count, rows, cols = parts.shape
+    lane = rows // 2
+    part = lane // 2
+
+    def kernel(p_ref, o_ref, held, send_sem, recv_sem):
+        me = lax.axis_index("wide")
+        place = ring_place(me, count)
+        at = lambda shift: ring_index((place + shift + 2 * count) % count, count)
+        peers = (at(1), at(-1))
+        ring_greet(*peers)
+
+        def copy(way, step, k):
+            sign = 1 if way == 0 else -1
+            span = pl.ds(k * part, part)
+            src = (
+                p_ref.at[at(-sign), pl.ds(way * lane + k * part, part)]
+                if step == 0
+                else held.at[way, step - 1, span]
+            )
+            return pltpu.make_async_remote_copy(
+                src_ref=src,
+                dst_ref=held.at[way, step, span],
+                send_sem=send_sem.at[way, step, k],
+                recv_sem=recv_sem.at[way, step, k],
+                device_id={"wide": peers[way]},
+                device_id_type=MESH,
+            )
+
+        for step in range(count - 1):
+            for k in range(2):
+                for way in range(2):
+                    sign = 1 if way == 0 else -1
+                    if step > 0:
+                        copy(way, step - 1, k).wait_recv()
+                        span = pl.ds(k * part, part)
+                        mine = p_ref[at(-sign * (1 + step)), pl.ds(way * lane + k * part, part)]
+                        held[way, step - 1, span] = (
+                            held[way, step - 1, span].astype(F32) + mine.astype(F32)
+                        ).astype(held.dtype)
+                    copy(way, step, k).start()
+        for k in range(2):
+            for way in range(2):
+                copy(way, count - 2, k).wait_recv()
+                rows_here = pl.ds(way * lane + k * part, part)
+                o_ref[rows_here] = held[way, count - 2, pl.ds(k * part, part)].astype(F32) + p_ref[
+                    me, rows_here
+                ].astype(F32)
+        for step in range(count - 1):
+            for k in range(2):
+                for way in range(2):
+                    copy(way, step, k).wait_send()
+
+    return pl.pallas_call(
+        kernel,
+        out_shape=jax.ShapeDtypeStruct((rows, cols), F32),
+        in_specs=[pl.BlockSpec(memory_space=pltpu.VMEM)],
+        out_specs=pl.BlockSpec(memory_space=pltpu.VMEM),
+        scratch_shapes=[
+            pltpu.VMEM((2, count - 1, lane, cols), parts.dtype),
+            pltpu.SemaphoreType.DMA((2, count - 1, 2)),
+            pltpu.SemaphoreType.DMA((2, count - 1, 2)),
+        ],
+        compiler_params=pltpu.CompilerParams(
+            collective_id=cid, has_side_effects=True, vmem_limit_bytes=40 * 2**20
+        ),
+    )(parts)
+
+
+TILE = 256
+
+def nt(a, b):
+    return lax.dot_general(a, b, (((1,), (1,)), ((), ())), preferred_element_type=F32)
+
+def tn(a, b):
+    return lax.dot_general(a, b, (((0,), (0,)), ((), ())), preferred_element_type=F32)
+
+def nn(a, b):
+    return jnp.dot(a, b, preferred_element_type=F32)
+
+def expert_pair(offsets, entry_all, grad_all, slots, slots_turned, gates, w_gate_up, w_down, earlier, first, pair, capacity):
+    count, tokens, width = entry_all.shape
+    ffe = w_down.shape[1]
+    local = w_down.shape[0]
+    room = count * capacity + TILE
+    most = count * capacity // TILE
+    adding = earlier is not None
+
+    def kernel(off_ref, e_ref, g_ref, s_ref, st_ref, gate_ref, wgu_ref, wd_ref, *rest):
+        if adding:
+            pc_ref, pb_ref = rest[:2]
+            rest = rest[2:]
+        c_ref, b_ref, pick_ref, dgu_ref, dd_ref, x_s, s_s, act_s, pg_s, cr_s, bk_s, gcol, pcol, sems = rest
+        e = pl.program_id(0)
+        if adding:
+            fetch = [
+                pltpu.make_async_copy(pc_ref, c_ref, sems.at[0]),
+                pltpu.make_async_copy(pb_ref, b_ref, sems.at[1]),
+            ]
+
+        @pl.when(e == 0)
+        def _():
+            if adding:
+                for f in fetch:
+                    f.start()
+            cr_s[...] = jnp.zeros_like(cr_s)
+            bk_s[...] = jnp.zeros_like(bk_s)
+            pcol[...] = jnp.zeros_like(pcol)
+
+        def start_of(expert, b):
+            return pl.multiple_of(off_ref[(first + expert) * (count + 1) + b], 16)
+
+        places = lax.broadcasted_iota(jnp.int32, (capacity, tokens), 0)
+        for b in range(count):
+            pick_out = places == s_ref[first + e, b : b + 1, :]
+            chosen = jnp.where(pick_out, 1.0, 0.0).astype(BF)
+            span = pl.ds(start_of(e, b), capacity)
+            x_s[span] = nn(chosen, e_ref[b]).astype(BF)
+            s_s[span] = nn(chosen, g_ref[b]).astype(BF)
+            gate_col = jnp.sum(
+                jnp.where(pick_out, gate_ref[first + e, b : b + 1, :], 0.0), axis=1, keepdims=True
+            )
+            gcol[span] = jnp.broadcast_to(gate_col, (capacity, 128))
+        total = start_of(e, count)
+        tail = pl.ds(total, TILE)
+        x_s[tail] = jnp.zeros((TILE, width), BF)
+        s_s[tail] = jnp.zeros((TILE, width), BF)
+        gcol[tail] = jnp.zeros((TILE, 128), F32)
+        tiles = (total + TILE - 1) // TILE
+
+        def step(i, carry):
+            rows = pl.ds(pl.multiple_of(i * TILE, TILE), TILE)
+            pre = nn(x_s[rows], wgu_ref[0])
+            gate_part = pre[:, :ffe]
+            up_part = pre[:, ffe:]
+            sig = jax.nn.sigmoid(gate_part)
+            swish = gate_part * sig
+            act = (swish * up_part).astype(BF)
+            act_s[rows] = act
+            result = nn(act, wd_ref[0]).astype(BF).astype(F32)
+            grad_rows = s_s[rows].astype(F32)
+            gate = gcol[rows][:, :1]
+            pcol[rows] = jnp.broadcast_to(
+                jnp.sum(result * grad_rows, axis=1, keepdims=True), (TILE, 128)
+            )
+            cr_s[e, rows] = (gate * result).astype(BF)
+            slot_grad = (gate * grad_rows).astype(BF)
+            s_s[rows] = slot_grad
+            act_grad = nt(slot_grad, wd_ref[0])
+            gate_grad = act_grad * up_part * sig * (1.0 + gate_part * (1.0 - sig))
+            pre_grad = jnp.concatenate([gate_grad, act_grad * swish], axis=1).astype(BF)
+            pg_s[rows] = pre_grad
+            bk_s[e, rows] = nt(pre_grad, wgu_ref[0]).astype(BF)
+            return carry
+
+        lax.fori_loop(0, tiles, step, 0)
+        for b in range(count):
+            pick_out = places == s_ref[first + e, b : b + 1, :]
+            span = pl.ds(start_of(e, b), capacity)
+            pick_ref[0, b : b + 1, :] = jnp.sum(
+                jnp.where(pick_out, pcol[span][:, :1], 0.0), axis=0, keepdims=True
+            )
+
+        @pl.when(tiles == 0)
+        def _():
+            dgu_ref[...] = jnp.zeros_like(dgu_ref)
+            dd_ref[...] = jnp.zeros_like(dd_ref)
+
+        block = 256
+        for k in range(1, most + 1):
+
+            @pl.when(tiles == k)
+            def _(k=k):
+                def columns(j, carry):
+                    cols = pl.ds(pl.multiple_of(j * block, block), block)
+                    dgu_ref[0, :, cols] = tn(x_s[: k * TILE], pg_s[: k * TILE, cols]).astype(BF)
+                    dd_ref[0, :, cols] = tn(act_s[: k * TILE], s_s[: k * TILE, cols]).astype(BF)
+                    return carry
+
+                lax.fori_loop(0, width // block, columns, 0)
+
+        @pl.when(e == pair - 1)
+        def _():
+            if adding:
+                for f in fetch:
+                    f.wait()
+            across = lax.broadcasted_iota(jnp.int32, (tokens, capacity), 1)
+            for b in range(count):
+                sum_c = sum_b = None
+                for x in range(pair):
+                    back = jnp.where(across == st_ref[b][:, first + x : first + x + 1], 1.0, 0.0).astype(BF)
+                    span = pl.ds(start_of(x, b), capacity)
+                    one_c, one_b = nn(back, cr_s[x, span]), nn(back, bk_s[x, span])
+                    sum_c = one_c if sum_c is None else sum_c + one_c
+                    sum_b = one_b if sum_b is None else sum_b + one_b
+                if adding:
+                    sum_c = sum_c + c_ref[b].astype(F32)
+                    sum_b = sum_b + b_ref[b].astype(F32)
+                c_ref[b] = sum_c.astype(BF)
+                b_ref[b] = sum_b.astype(BF)
+
+    once = pl.Buffered(1)
+    whole = lambda shape: pl.BlockSpec(shape, lambda e, off: (0,) * len(shape), pipeline_mode=once)
+    any_space = pl.BlockSpec(memory_space=pl.ANY)
+    cube = (count, tokens, width)
+    in_specs = [
+        whole(cube), whole(cube), whole(slots.shape), whole(slots_turned.shape), whole(gates.shape),
+        pl.BlockSpec((1, width, 2 * ffe), lambda e, off: (first + e, 0, 0)),
+        pl.BlockSpec((1, ffe, width), lambda e, off: (first + e, 0, 0)),
+    ]
+    operands = [entry_all, grad_all, slots, slots_turned, gates, w_gate_up, w_down]
+    if adding:
+        in_specs += [any_space, any_space]
+        operands += list(earlier)
+    return pl.pallas_call(
+        kernel,
+        grid_spec=pltpu.PrefetchScalarGridSpec(
+            num_scalar_prefetch=1,
+            grid=(pair,),
+            in_specs=in_specs,
+            out_specs=[
+                whole(cube), whole(cube),
+                pl.BlockSpec((1, count, tokens), lambda e, off: (e, 0, 0)),
+                pl.BlockSpec((1, width, 2 * ffe), lambda e, off: (e, 0, 0)),
+                pl.BlockSpec((1, ffe, width), lambda e, off: (e, 0, 0)),
+            ],
+            scratch_shapes=[
+                pltpu.VMEM((room, width), BF),
+                pltpu.VMEM((room, width), BF),
+                pltpu.VMEM((room, ffe), BF),
+                pltpu.VMEM((room, 2 * ffe), BF),
+                pltpu.VMEM((pair, room, width), BF),
+                pltpu.VMEM((pair, room, width), BF),
+                pltpu.VMEM((room, 128), F32),
+                pltpu.VMEM((room, 128), F32),
+                pltpu.SemaphoreType.DMA((2,)),
+            ],
+        ),
+        out_shape=[
+            jax.ShapeDtypeStruct(cube, BF),
+            jax.ShapeDtypeStruct(cube, BF),
+            jax.ShapeDtypeStruct((pair, count, tokens), F32),
+            jax.ShapeDtypeStruct((pair, width, 2 * ffe), BF),
+            jax.ShapeDtypeStruct((pair, ffe, width), BF),
+        ],
+        compiler_params=pltpu.CompilerParams(
+            dimension_semantics=("arbitrary",), vmem_limit_bytes=60 * 2**20
+        ),
+        cost_estimate=pl.CostEstimate(
+            flops=pair * count * capacity * 6 * width * ffe * 3, bytes_accessed=40 * 2**20, transcendentals=0
+        ),
+    )(offsets, *operands)
+
+
+def pair_sum(parts):
+    here = lax.axis_index("narrow")
+    chip, core = here // 2, here % 2
+    to_core = [(0, 1), (1, 0), (2, 3), (3, 2)]
+    to_chip = [(0, 2), (2, 0), (1, 3), (3, 1)]
+    pick = lambda array, index, axis: lax.dynamic_index_in_dim(array, index, axis, keepdims=False)
+    add = lambda one, two: (one.astype(F32) + two.astype(F32)).astype(BF)
+    cubes = [p.reshape(p.shape[0], 2, 2, p.shape[1] // 4, p.shape[2]) for p in parts]
+    got = [lax.ppermute(pick(c, 1 - core, 2), "narrow", to_core) for c in cubes]
+    half = [add(pick(c, core, 2), g) for c, g in zip(cubes, got)]
+    got = [lax.ppermute(pick(h, 1 - chip, 1), "narrow", to_chip) for h in half]
+    own = [add(pick(h, chip, 1), g) for h, g in zip(half, got)]
+    other = [lax.ppermute(o, "narrow", to_chip) for o in own]
+    done = []
+    for o, t in zip(own, other):
+        mine = jnp.stack([jnp.where(chip == 0, o, t), jnp.where(chip == 0, t, o)], axis=1)
+        theirs = lax.ppermute(mine, "narrow", to_core)
+        both = jnp.stack([jnp.where(core == 0, mine, theirs), jnp.where(core == 0, theirs, mine)], axis=2)
+        done.append(both.reshape(o.shape[0], 4 * o.shape[1], o.shape[2]).astype(F32))
+    return done
+
+
+def narrow_sum(parts):
+    if lax.axis_size("narrow") == 4:
+        return pair_sum(parts)
+    return [lax.psum(p, "narrow").astype(F32) for p in parts]
+
+
 def local(
     hidden,
     lengths,
@@ -139,6 +508,7 @@
 ):
     rows_here = hidden.shape[1]
     width = hidden.shape[2]
+    wide = lax.axis_size("wide")
     seq_len = rows_here * lax.axis_size("narrow")
     head_dim = HEAD_DIM
     group_size = HEADS // KV_HEADS
@@ -152,6 +522,32 @@
     offset = lax.axis_index("narrow") * rows_here
     local_places = offset + jnp.arange(rows_here, dtype=jnp.int32)
     valid = (local_places < length_here).astype(jnp.float32)[:, None]
+    grad_all = lax.all_gather(cotangent[0], "wide", axis=0)
+    picks = routes.shape[2]
+    expert_total = w_router.shape[1]
+    expert_here = w_gate_up.shape[0]
+    first_expert = lax.axis_index("wide") * expert_here
+    capacity = 2 * rows_here * picks // expert_total
+    labels = jnp.concatenate(
+        [routes[0].T, jnp.broadcast_to(lengths[0], (1, rows_here)).astype(jnp.int32)], axis=0
+    )
+    labels_all = lax.all_gather(labels, "wide", axis=0)
+    routes_all = labels_all[:, :picks]
+    valid_all = local_places[None, None, :] < labels_all[:, picks:]
+    experts = jnp.arange(expert_total, dtype=jnp.int32)
+    member_all = jnp.any(routes_all[:, :, None, :] == experts[None, None, :, None], axis=1)
+    member_here = lax.dynamic_slice_in_dim(member_all, first_expert, expert_here, 1) & valid_all
+    upper = jnp.triu(jnp.ones((rows_here, rows_here), BF))
+    reached = jnp.einsum(
+        "bet,ts->bes", member_here.astype(BF), upper, preferred_element_type=F32
+    ).astype(jnp.int32)
+    slots = jnp.where(member_here, reached - 1, -1).transpose(1, 0, 2)
+    slots_turned = slots.transpose(1, 2, 0)
+    padded = (reached[:, :, -1].T + 15) // 16 * 16
+    offsets = jnp.concatenate(
+        [jnp.zeros((expert_here, 1), jnp.int32), jnp.cumsum(padded, axis=1)], axis=1
+    ).reshape(-1)
+
     source = hidden[0].astype(jnp.float32)
     normed, scale_one = norm_forward(source, attn_gain)
     normed_low = normed.astype(jnp.bfloat16)
@@ -185,9 +581,8 @@
     )
     context, log_sums = attend_forward(queries, keys_low, values_low, length_here, scaling)
     context_rows = context.transpose(0, 3, 1, 2, 4).reshape(seq_len, query_cols)
-    piece = context_rows
     attn_part = lax.psum_scatter(
-        jnp.dot(piece, w_out, preferred_element_type=jnp.float32).astype(jnp.bfloat16),
+        jnp.dot(context_rows, w_out, preferred_element_type=jnp.float32).astype(jnp.bfloat16),
         "narrow",
         scatter_dimension=0,
         tiled=True,
@@ -195,91 +590,45 @@
     mixed = source + attn_part
     normed_two, scale_two = norm_forward(mixed, moe_gain)
     entry = normed_two.astype(jnp.bfloat16)
-    logits = jnp.dot(entry, w_router, preferred_element_type=jnp.float32)
-    route_here = routes[0]
-    tokens_here, picks = route_here.shape
-    expert_total = w_router.shape[1]
-    capacity = 2 * tokens_here * picks // expert_total
-    member = (
-        route_here[:, :, None] == jnp.arange(expert_total, dtype=jnp.int32)[None, None, :]
-    ).astype(jnp.int32)
-    flat_member = member.reshape(tokens_here * picks, expert_total)
-    earlier = jnp.cumsum(flat_member, axis=0) - flat_member
-    slot_index = jnp.sum(earlier * flat_member, axis=1)
-    places = route_here.reshape(-1) * capacity + slot_index
-    member_float = member.astype(jnp.float32)
-    chosen = jnp.einsum("tke,te->tk", member_float, logits, precision=HIGHEST)
-    highest = jnp.max(chosen, axis=-1, keepdims=True)
-    raised = jnp.exp(chosen - highest)
-    shares = raised / jnp.sum(raised, axis=-1, keepdims=True)
-    gates = shares * valid
-    outgoing = (
-        jnp.zeros((expert_total * capacity, width), jnp.bfloat16)
-        .at[places]
-        .set(jnp.repeat(entry, picks, axis=0))
-    )
-    received = lax.all_to_all(
-        outgoing.reshape(expert_total, capacity, width),
-        "wide",
-        split_axis=0,
-        concat_axis=1,
-        tiled=True,
-    )
-    expert_pre = jnp.einsum("erd,edf->erf", received, w_gate_up, preferred_element_type=jnp.float32)
-    ffe_width = w_down.shape[1]
-    gate_part = expert_pre[..., :ffe_width]
-    up_part = expert_pre[..., ffe_width:]
-    sigmoid_gate = jax.nn.sigmoid(gate_part)
-    swish = gate_part * sigmoid_gate
-    act_low = (swish * up_part).astype(jnp.bfloat16)
-    expert_result = jnp.einsum(
-        "erf,efd->erd", act_low, w_down, preferred_element_type=jnp.float32
-    ).astype(jnp.bfloat16)
-    returned = lax.all_to_all(expert_result, "wide", split_axis=1, concat_axis=0, tiled=True)
-    picked = returned.reshape(expert_total * capacity, width)[places].reshape(
-        tokens_here, picks, width
-    )
-    expert_sum = jnp.einsum("tk,tkd->td", gates, picked, precision=HIGHEST)
+
+    entry_all = ring_gather(entry, wide, 1)
+    logits = jnp.einsum("btd,de->bet", entry_all, w_router, preferred_element_type=F32)
+    masked = jnp.where(member_all, logits, -jnp.inf)
+    raised = jnp.exp(masked - jnp.max(masked, axis=1, keepdims=True))
+    shares_all = raised / jnp.sum(raised, axis=1, keepdims=True)
+    gates = (
+        lax.dynamic_slice_in_dim(shares_all, first_expert, expert_here, 1) * valid_all.astype(F32)
+    ).transpose(1, 0, 2)
+    pair = min(2, expert_here)
+    earlier, pick_parts, weight_parts = None, [], []
+    for first in range(0, expert_here, pair):
+        expert_part, back_part, pick_part, up_part, down_part = expert_pair(
+            offsets, entry_all, grad_all, slots, slots_turned, gates, w_gate_up, w_down,
+            earlier, first, pair, capacity,
+        )
+        earlier = (expert_part, back_part)
+        pick_parts.append(pick_part)
+        weight_parts.append((up_part, down_part))
+    entry_home = ring_scatter(back_part, 2)
+    pick_home = lax.all_to_all(
+        jnp.concatenate(pick_parts, axis=0), "wide", split_axis=1, concat_axis=0, tiled=True
+    ).reshape(expert_total, rows_here)
+    summed = [narrow_sum(p) for p in weight_parts]
+    gate_up_grad = jnp.concatenate([s[0] for s in summed], axis=0)
+    down_grad = jnp.concatenate([s[1] for s in summed], axis=0)
+
+    expert_part, entry_home = lax.optimization_barrier((expert_part, entry_home))
+    expert_sum = lax.psum_scatter(expert_part, "wide", scatter_dimension=0, tiled=False).astype(F32)
     output_rows = (valid * (mixed + expert_sum)).astype(jnp.bfloat16)
     grad_rows_here = cotangent[0].astype(jnp.float32) * valid
-    slot_grad = (gates[:, :, None] * grad_rows_here[:, None, :]).astype(jnp.bfloat16)
-    grad_outgoing = (
-        jnp.zeros((expert_total * capacity, width), jnp.bfloat16)
-        .at[places]
-        .set(slot_grad.reshape(tokens_here * picks, width))
-    )
-    grad_received = lax.all_to_all(
-        grad_outgoing.reshape(expert_total, capacity, width),
-        "wide",
-        split_axis=0,
-        concat_axis=1,
-        tiled=True,
-    )
-    act_grad = jnp.einsum("erd,efd->erf", grad_received, w_down, preferred_element_type=jnp.float32)
-    down_grad = jnp.einsum(
-        "erf,erd->efd", act_low, grad_received, preferred_element_type=jnp.float32
-    )
-    gate_grad = act_grad * up_part * sigmoid_gate * (1.0 + gate_part * (1.0 - sigmoid_gate))
-    pre_grad = jnp.concatenate([gate_grad, act_grad * swish], axis=-1).astype(jnp.bfloat16)
-    gate_up_grad = jnp.einsum(
-        "erd,erf->edf", received, pre_grad, preferred_element_type=jnp.float32
-    )
-    entry_back = jnp.einsum(
-        "erf,edf->erd", pre_grad, w_gate_up, preferred_element_type=jnp.float32
-    ).astype(jnp.bfloat16)
-    entry_home = lax.all_to_all(entry_back, "wide", split_axis=1, concat_axis=0, tiled=True)
-    entry_rows = entry_home.reshape(expert_total * capacity, width)[places].reshape(
-        tokens_here, picks, width
-    )
-    entry_grad = jnp.sum(entry_rows, axis=1, dtype=jnp.float32)
-    pick_grad = jnp.einsum("td,tkd->tk", grad_rows_here, picked, precision=HIGHEST) * valid
-    chosen_grad = shares * (pick_grad - jnp.sum(shares * pick_grad, axis=-1, keepdims=True))
-    logit_grad = jnp.einsum("tk,tke->te", chosen_grad, member_float, precision=HIGHEST)
+
+    shares = lax.dynamic_index_in_dim(shares_all, lax.axis_index("wide"), 0, keepdims=False)
+    logit_grad = shares * (pick_home - jnp.sum(shares * pick_home, axis=0, keepdims=True))
     router_grad = lax.dot_general(
-        entry.astype(jnp.float32), logit_grad, (((0,), (0,)), ((), ())), precision=HIGHEST
-    )
-    entry_grad = entry_grad + lax.dot_general(
-        logit_grad, w_router.astype(jnp.float32), (((1,), (1,)), ((), ())), precision=HIGHEST
+        entry.astype(jnp.float32), logit_grad, (((0,), (1,)), ((), ())), precision=HIGHEST
+    )
+    entry_grad = entry_home + lax.dot_general(
+        logit_grad, w_router.astype(jnp.float32), (((0,), (1,)), ((), ())), precision=HIGHEST
     )
     mixed_from_norm, gain_two_grad = norm_backward(mixed, scale_two, moe_gain, entry_grad)
     mixed_grad = grad_rows_here + mixed_from_norm
@@ -316,10 +665,9 @@
     qkv_weight_grad = lax.dot_general(
         whole, qkv_grad, (((0,), (0,)), ((), ())), preferred_element_type=jnp.float32
     )
-    piece = qkv_grad
     normed_grad = lax.psum_scatter(
         lax.dot_general(
-            piece, w_qkv, (((1,), (1,)), ((), ())), preferred_element_type=jnp.float32
+            qkv_grad, w_qkv, (((1,), (1,)), ((), ())), preferred_element_type=jnp.float32
         ).astype(jnp.bfloat16),
         "narrow",
         scatter_dimension=0,
@@ -327,19 +675,15 @@
     ).astype(jnp.float32)
     source_from_norm, gain_one_grad = norm_backward(source, scale_one, attn_gain, normed_grad)
     grad_input = (mixed_grad + source_from_norm).astype(jnp.bfloat16)
-    gate_up_grad, down_grad, router_grad, gain_one_grad, gain_two_grad = (
-        lax.psum(gate_up_grad.astype(jnp.bfloat16), "narrow").astype(jnp.float32),
-        lax.psum(down_grad.astype(jnp.bfloat16), "narrow").astype(jnp.float32),
-        lax.psum(router_grad.astype(jnp.bfloat16), "narrow").astype(jnp.float32),
-        lax.psum(gain_one_grad.astype(jnp.bfloat16), "narrow").astype(jnp.float32),
-        lax.psum(gain_two_grad.astype(jnp.bfloat16), "narrow").astype(jnp.float32),
-    )
-    qkv_weight_grad, out_grad, router_grad, gain_one_grad, gain_two_grad = (
+    gain_one_grad = jnp.sum(qkv_weight_grad * w_qkv.astype(F32), axis=1) / attn_gain
+    small = jnp.concatenate([router_grad, gain_one_grad[:, None], gain_two_grad[:, None]], axis=1)
+    small = lax.psum(small, ("wide", "narrow"))
+    router_grad = small[:, :expert_total]
+    gain_one_grad = small[:, expert_total]
+    gain_two_grad = small[:, expert_total + 1]
+    qkv_weight_grad, out_grad = (
         lax.psum(qkv_weight_grad.astype(jnp.bfloat16), "wide").astype(jnp.float32),
         lax.psum(out_grad.astype(jnp.bfloat16), "wide").astype(jnp.float32),
-        lax.psum(router_grad.astype(jnp.bfloat16), "wide").astype(jnp.float32),
-        lax.psum(gain_one_grad.astype(jnp.bfloat16), "wide").astype(jnp.float32),
-        lax.psum(gain_two_grad.astype(jnp.bfloat16), "wide").astype(jnp.float32),
     )
     query_weight_grad = qkv_weight_grad[:, :query_cols]
     key_weight_grad = qkv_weight_grad[:, query_cols : query_cols + key_cols]

time: 1390 us -> 676 us (0.49)
  waiting for transfers between devices: 924 us -> 247 us
  Pallas kernels: 0 us -> 193 us
  matrix products: 165 us -> 47.4 us
  local copies, waits for them, and re-layouts: 141 us -> 45.2 us
    all_to_all x4 -> x1, waiting for transfers between devices: 644 us -> 0.01 us  [local(): lax.all_to_all(jnp.concatenate(pick_parts, axis=0), 'wide', split_axis=1,...]
    pallas_call x0 -> x4, Pallas kernels: none -> 193 us  [the longest x2 83.1 us: expert_pair(): pl.pallas_call(kernel, grid_spec=pltpu.PrefetchScalarGridSpec(num_scalar_...]
    psum x1, waiting for transfers between devices: 171 us -> 0.01 us  [local(): small = lax.psum(small, ('wide', 'narrow'))]
    ppermute x0 -> x16, waiting for transfers between devices: none -> 133 us  [the longest x4 83.7 us: pair_sum(): other = [lax.ppermute(o, 'narrow', to_chip) for o in own]]
    dot_general x15 -> x6, matrix products: 115 us -> 11 us  [the longest x1 3.51 us: local(): jnp.einsum('btd,de->bet', entry_all, w_router, preferred_element_type=F32)]
    all_to_all x4 -> x0, local copies, waits for them, and re-layouts: 36.5 us -> none  [the longest x1 9.96 us: local(): lax.all_to_all(entry_back, 'wide', split_axis=1, concat_axis=0, tiled=True)]
    convert_element_type x2 -> x0, local copies, waits for them, and re-layouts: 35 us -> none  [the longest x1 22.8 us: local(): expert_result = jnp.einsum('erf,efd->erd', act_low, w_down, preferred_ele...]
    gather x2 -> x0, local copies, waits for them, and re-layouts: 31.6 us -> none  [the longest x1 15.9 us: local(): entry_home.reshape(expert_total * capacity, width)[places]]
  transfers between devices with their start and end apart: 10 -> 25, of which waited for: 9 -> 10; matrix products, arithmetic and copies ran while one was open for 15% -> 13% of each run, Pallas kernels for 0% -> 16%
where the time goes in v1:
time: 676 us; the launch traced here: 674 us
  waiting for transfers between devices  247 us (37%)
  Pallas kernels  193 us (29%)
  other arithmetic  71.6 us (11%)
  matrix products  47.4 us (7%)
  local copies, waits for them, and re-layouts  45.2 us (7%)
  blocking collectives  31.5 us (5%)
  starting transfers between devices  20.5 us (3%)
  between operations  17.6 us (3%)
    ppermute x4, waiting for transfers between devices, pair_sum(): other = [lax.ppermute(o, 'narrow', to_chip) for o in own]  83.7 us
    pallas_call x2, Pallas kernels, expert_pair(): pl.pallas_call(kernel, grid_spec=pltpu.PrefetchScalarGridSpec(num_scalar_...  83.1 us
    pallas_call x1, Pallas kernels, ring_gather(): pl.pallas_call(kernel, out_shape=jax.ShapeDtypeStruct((count, rows, cols)...  69.7 us
    psum x1, waiting for transfers between devices, local(): lax.psum(qkv_weight_grad.astype(jnp.bfloat16), 'wide').astype(jnp.float32)  69.4 us
    ppermute x4, waiting for transfers between devices, pair_sum(): got = [lax.ppermute(pick(h, 1 - chip, 1), 'narrow', to_chip) for h in half]  47.6 us
    pallas_call x1, Pallas kernels, ring_scatter(): pl.pallas_call(kernel, out_shape=jax.ShapeDtypeStruct((rows, cols), F32),...  40.7 us
    all_gather x1, blocking collectives, local(): labels_all = lax.all_gather(labels, 'wide', axis=0)  31.5 us
    all_gather x1, waiting for transfers between devices, local(): whole = lax.all_gather(normed_low, 'narrow', axis=0, tiled=True)  23.6 us
  transfers between devices with their start and end apart: 25, of which 10 were waited for; matrix products, arithmetic and copies ran while one was open for 13% of the time, Pallas kernels for 16%

profile of v1, /device:TPU:0, one launch (start us, length us, event | category | flops | bytes accessed | tf_op | source)
XLA Modules:
  0.0 674.2 jit_solution(13262256482542705358)
XLA Ops:
  14.0 23.6 %all-gather.6.cloned.1.call-done = bf16[1024,1024]{1,0:T(8,128)(2,1)} async-done(((bf16[256,1024]{1,0:T(8,128)(2,1)}), bf16[1024,1024]{1,0:T(8,128)(2,1)}) %all-gather.6.cloned.1.call-update) | async-done | bytes 2097168 | tf_op jit(solution)/shard_map/all_gather | solution.py:554
  37.5 2.9 fusion.102
  42.0 18.7 %while.30 = (s32[]{:T(128)}, bf16[2,2,2,512,64]{3,4,2,1,0:T(8,128)(2,1)S(1)}, f32[2,2,2,512]{3,2,1,0:T(2,128)S(1)}, s32[2]{0:T(128)S(1)}, s32[]{:T(128)}, /*inde...) while((s32[]{:T(128)}, ...), condition=%wide.region_4.5_spmd.clone.clone, body=%wide.region_1.4_spmd.clone.clone.sunk | while | flops 563215872 | bytes 28383364 | solution.py:79
  48.3 3.0 fusion.144
  57.7 3.0 fusion.144
  64.8 31.5 %all-gather.1 = s32[8,9,256]{2,1,0:T(8,128)S(1)} all-gather(s32[1,9,256]{2,1,0:T(8,128)S(1)} %pad_bitcast_fusion), channel_id=2, replica_groups=mesh['wide'=8,'narrow'=4] {'wide'}, dimensions={0}, use_global_device_ids=true | all-gather | bytes 82944 | tf_op jit(solution)/shard_map/all_gather | solution.py:534
  106.8 69.7 %shard_map.212.e_ref = bf16[8,256,1024]{2,1,0:T(8,128)(2,1)} custom-call(bf16[256,1024]{1,0:T(8,128)(2,1)} %multiply_convert_fusion.1.x_ref), custom_call_target="tpu_custom_call" | custom-call | tf_op jit(solution)/shard_map/pallas_call | solution.py:199
  176.6 3.5 fusion.87
  181.4 35.0 %shard_map.213 = (bf16[8,256,1024]{2,1,0:T(8,128)(2,1)}, bf16[8,256,1024]{2,1,0:T(8,128)(2,1)}, f32[2,8,256]{2,1,0:T(8,128)}, bf16[2,1024,1024]{2,1,0:T(8,128)(2,1)}, bf16[2,512,1024]{2,1,0:T(8,128)(2,1)}) custom-call(s32[36]{0:T(128)} %reshape.318.off_ref, bf16[8,256,1024]{2,1,0:T(8,128)(2,1)} %shard_map.212.e_ref, ...), custom_call_target="tpu_custom_call" | custom-call | flops 19327352832 | bytes 41943040 | tf_op jit(solution)/shard_map/pallas_call | solution.py:426
  216.4 48.0 %shard_map.214 = (bf16[8,256,1024]{2,1,0:T(8,128)(2,1)}, bf16[8,256,1024]{2,1,0:T(8,128)(2,1)}, f32[2,8,256]{2,1,0:T(8,128)}, bf16[2,1024,1024]{2,1,0:T(8,128)(2,1)}, bf16[2,512,1024]{2,1,0:T(8,128)(2,1)}) custom-call(s32[36]{0:T(128)} %reshape.318.off_ref, bf16[8,256,1024]{2,1,0:T(8,128)(2,1)} %shard_map.212.e_ref, ...), custom_call_target="tpu_custom_call" | custom-call | flops 19327352832 | bytes 41943040 | tf_op jit(solution)/shard_map/pallas_call | solution.py:426
  265.8 12.7 %all-to-all-start = ((f32[4,8,256]{2,0,1:T(4,128)}), f32[4,8,256]{2,0,1:T(4,128)S(1)}, u32[]{:S(2)}, u32[]{:S(2)}) async-start(f32[4,8,256]{2,0,1:T(4,128)} %copy.137), calls=%async_computation.2 | async-start | bytes 65536 | tf_op jit(solution)/shard_map/all_to_all | solution.py:613
  280.7 40.7 %shard_map.215 = f32[256,1024]{1,0:T(8,128)S(1)} custom-call(bf16[8,256,1024]{2,1,0:T(8,128)(2,1)S(1)} %copy-done.2), custom_call_target="tpu_custom_call" | custom-call | tf_op jit(solution)/shard_map/pallas_call | solution.py:265
  327.1 20.0 %all-gather.10.cloned.1.call-done = bf16[1024,1024]{1,0:T(8,128)(2,1)} async-done(((bf16[256,1024]{1,0:T(8,128)(2,1)}), bf16[1024,1024]{1,0:T(8,128)(2,1)}) %all-gather.10.cloned.1.call-update) | async-done | bytes 2097168 | tf_op jit(solution)/shard_map/all_gather | solution.py:636
  350.5 25.6 %while.31 = (s32[]{:T(128)}, f32[2,1024,64]{1,2,0:T(8,128)S(1)}, f32[2,1024,64]{1,2,0:T(8,128)S(1)}, f32[2,2,2,512,64]{3,4,2,1,0:T(8,128)}, s32[2]{0:T(128)S(1)}...) while((s32[]{:T(128)}, f32[2,1024,64]{1,2,0:T(8,128)S(1)}, ...), condition=%wide.region_16.17_spmd.clone.clone, body=%wide.region_14.16_spmd.clone.clone.sunk | while | flops 1364983296 | bytes 76855528 | solution.py:122
  354.2 3.7 multiply_reduce_fusion.6
  366.9 3.7 multiply_reduce_fusion.6
  382.6 3.1 convolution_convert_fusion.3
  385.8 2.6 convolution_convert_fusion
  388.7 2.7 constant_dynamic-slice_fusion.3
  406.6 2.7 fusion.49
  411.7 2.6 fusion.48
  414.7 9.0 %collective-permute-done.9 = bf16[2,128,1024]{2,1,0:T(8,128)(2,1)S(1)} collective-permute-done((bf16[2,128,1024]{2,1,0:T(8,128)(2,1)S(1)}, bf16[2,128,1024]{2,1,0:T(8,128)(2,1)S(1)}, u32[]{:S(2)}, u32[]{:S(2)}) %collective-permute-start.9) | collective-permute-done | bytes 524320 | tf_op jit(solution)/shard_map/ppermute | solution.py:476
  424.4 38.5 %collective-permute-done.13 = bf16[2,128,1024]{2,1,0:T(8,128)(2,1)S(1)} collective-permute-done((bf16[2,128,1024]{2,1,0:T(8,128)(2,1)S(1)}, bf16[2,128,1024]{2,1,0:T(8,128)(2,1)S(1)}, u32[]{:S(2)}, u32[]{:S(2)}) %collective-permute-start.13) | collective-permute-done | bytes 524320 | tf_op jit(solution)/shard_map/ppermute | solution.py:476
  465.6 31.2 %collective-permute-done.10 = bf16[2,128,1024]{2,1,0:T(8,128)(2,1)S(1)} collective-permute-done((bf16[2,128,1024]{2,1,0:T(8,128)(2,1)S(1)}, bf16[2,128,1024]{2,1,0:T(8,128)(2,1)S(1)}, u32[]{:S(2)}, u32[]{:S(2)}) %collective-permute-start.10) | collective-permute-done | bytes 524320 | tf_op jit(solution)/shard_map/ppermute | solution.py:478
  497.9 10.2 %collective-permute-done.14 = bf16[2,128,1024]{2,1,0:T(8,128)(2,1)S(1)} collective-permute-done((bf16[2,128,1024]{2,1,0:T(8,128)(2,1)S(1)}, bf16[2,128,1024]{2,1,0:T(8,128)(2,1)S(1)}, u32[]{:S(2)}, u32[]{:S(2)}) %collective-permute-start.14) | collective-permute-done | bytes 524320 | tf_op jit(solution)/shard_map/ppermute | solution.py:478
  508.3 22.6 %collective-permute-done.2 = bf16[2,256,1024]{2,1,0:T(8,128)(2,1)S(1)} collective-permute-done((bf16[2,256,1024]{2,1,0:T(8,128)(2,1)S(1)}, bf16[2,256,1024]{2,1,0:T(8,128)(2,1)S(1)}, u32[]{:S(2)}, u32[]{:S(2)}) %collective-permute-start.2) | collective-permute-done | bytes 1048608 | tf_op jit(solution)/shard_map/ppermute | solution.py:478
  533.1 19.7 %collective-permute-done.6 = bf16[2,256,1024]{2,1,0:T(8,128)(2,1)S(1)} collective-permute-done((bf16[2,256,1024]{2,1,0:T(8,128)(2,1)S(1)}, bf16[2,256,1024]{2,1,0:T(8,128)(2,1)S(1)}, u32[]{:S(2)}, u32[]{:S(2)}) %collective-permute-start.6) | collective-permute-done | bytes 1048608 | tf_op jit(solution)/shard_map/ppermute | solution.py:478
  555.5 3.9 maximum_convert_fusion.1
  562.5 69.4 %all-reduce.8.cloned.1.call-done = (bf16[1024,512]{0,1:T(8,128)(2,1)}, bf16[256,1024]{1,0:T(8,128)(2,1)}) async-done(((bf16[1024,512]{0,1:T(8,128)(2,1)}, bf16[256,1024]{1,0:T(8,128)(2,1)}), (bf16[1024,512]{0,1:T(8,128)(2,1)}, bf16[256,1024]{1,0:T(8,128)(2,1)})) %all-reduce.8.cloned.1.call-update) | async-done | bytes 1572880 | tf_op jit(solution)/shard_map/psum | solution.py:685
  635.2 2.5 copy.150
  651.2 10.8 %maximum_convert_fusion = f32[4,1024,1024]{2,1,0:T(8,128)} fusion(bf16[2,1024,1024]{2,1,0:T(8,128)(2,1)} %bitcast.342, bf16[2,1024,1024]{2,1,0:T(8,128)(2,1)} %bitcast.341), kind=kLoop, calls=%fused_computation.58 | loop fusion | flops 8388608 | bytes 25165824 | tf_op jit(solution)/shard_map/concatenate | solution.py:617
  663.5 3.1 fusion.75
  (313 shorter events, 120.7 us)
Async XLA Ops:
  8.0 53.4 %copy-start = (bf16[256,1024]{1,0:T(8,128)(2,1)S(1)}, bf16[256,1024]{1,0:T(8,128)(2,1)}, u32[]{:S(2)}) copy-start(bf16[256,1024]{1,0:T(8,128)(2,1)} %param.25) | copy-start | bytes 1572868
  8.1 29.5 %all-gather.6.cloned.1.call-start = ((), (), s32[]{:S(2)}) async-start(), calls=%async_computation.4 | async-start | bytes 2621440 | tf_op jit(solution)/shard_map/all_gather | solution.py:554
  12.1 91.4 %reduce-scatter.4.cloned.1.call-start = ((), (), s32[]{:S(2)}) async-start(), calls=%async_computation.5 | async-start | bytes 2621440 | tf_op jit(solution)/shard_map/reduce_scatter | solution.py:584
  12.3 28.1 %copy-start.35 = (bf16[1024,128]{0,1:T(8,128)(2,1)}, bf16[1024,128]{0,1:T(8,128)(2,1)S(1)}, u32[]{:S(2)}) copy-start(bf16[1024,128]{0,1:T(8,128)(2,1)S(1)} %copy.123) | copy-start | bytes 786436
  12.7 27.7 %copy-start.30 = (bf16[1024,256]{0,1:T(8,128)(2,1)}, bf16[1024,256]{0,1:T(8,128)(2,1)S(1)}, u32[]{:S(2)}) copy-start(bf16[1024,256]{0,1:T(8,128)(2,1)S(1)} %copy.122) | copy-start | bytes 1572868
  63.5 117.9 %all-gather.8.cloned.1.call-start = ((), (), s32[]{:S(2)}) async-start(), calls=%async_computation.6 | async-start | bytes 4718592 | tf_op jit(solution)/shard_map/all_gather | solution.py:525
  104.8 71.8 %copy-start.42 = (f32[256]{0:T(256)}, f32[256]{0:T(256)S(1)}, u32[]{:S(2)}) copy-start(f32[256]{0:T(256)S(1)} %add_rsqrt_fusion) | copy-start | bytes 3076
  106.8 69.7 %copy-start.32 = (bf16[1024,32]{0,1:T(8,128)(2,1)S(1)}, bf16[1024,32]{0,1:T(8,128)(2,1)}, u32[]{:S(2)}) copy-start(bf16[1024,32]{0,1:T(8,128)(2,1)} %param.27) | copy-start | bytes 196612
  216.4 48.0 %copy-start.44 = (f32[2,8,256]{2,1,0:T(8,128)S(1)}, f32[2,8,256]{2,1,0:T(8,128)}, u32[]{:S(2)}) copy-start(f32[2,8,256]{2,1,0:T(8,128)} %get-tuple-element.148) | copy-start | bytes 49156
  265.8 55.7 %all-to-all-start = ((f32[4,8,256]{2,0,1:T(4,128)}), f32[4,8,256]{2,0,1:T(4,128)S(1)}, u32[]{:S(2)}, u32[]{:S(2)}) async-start(f32[4,8,256]{2,0,1:T(4,128)} %copy.137), calls=%async_computation.2 | async-start | bytes 65536 | tf_op jit(solution)/shard_map/all_to_all | solution.py:613
  278.5 68.6 %all-gather.10.cloned.1.call-start = ((), (), s32[]{:S(2)}) async-start(), calls=%async_computation.8 | async-start | bytes 2621440 | tf_op jit(solution)/shard_map/all_gather | solution.py:636
  280.7 40.8 %copy-start.5 = (bf16[256,1024]{1,0:T(8,128)(2,1)S(1)}, bf16[256,1024]{1,0:T(8,128)(2,1)}, u32[]{:S(2)}) copy-start(bf16[256,1024]{1,0:T(8,128)(2,1)} %reduce-scatter.4.cloned.1.call-done) | copy-start | bytes 1572868
  326.3 233.2 %all-reduce.6.cloned.1.call-start = ((), (), s32[]{:S(2)}) async-start(), calls=%async_computation.10 | async-start | bytes 327680 | tf_op jit(solution)/shard_map/psum | solution.py:680
  382.6 249.3 %all-reduce.8.cloned.1.call-start = ((), (), s32[]{:S(2)}) async-start(), calls=%async_computation.11 | async-start | bytes 3145728 | tf_op jit(solution)/shard_map/psum | solution.py:685
  385.7 276.3 %reduce-scatter.8.cloned.1.call-start = ((), (), s32[]{:S(2)}) async-start(), calls=%async_computation.9 | async-start | bytes 2621440 | tf_op jit(solution)/shard_map/reduce_scatter | solution.py:668
  388.4 275.0 %reduce-scatter.6.cloned.1.call-start = ((), (), s32[]{:S(2)}) async-start(), calls=%async_computation.7 | async-start | bytes 4718592 | tf_op jit(solution)/shard_map/reduce_scatter | solution.py:621
  392.9 13.7 %collective-permute-start = (bf16[2,2,256,1024]{3,2,0,1:T(8,128)(2,1)}, bf16[2,2,256,1024]{3,2,0,1:T(8,128)(2,1)}, u32[]{:S(2)}, u32[]{:S(2)}) collective-permute-start(bf16[2,2,256,1024]{3,2,0,1:T(8,128)(2,1)} %bitcast.296), channel_id=1, source_target_pairs={{0,1},{1,0},{2,3},{3,2},{4,5},{5,4},{6,7},{7,6},{8,9},{9,8},{10,11... | collective-permute-start | bytes 6291464 | tf_op jit(solution)/shard_map/ppermute | solution.py:474
  396.0 4.5 collective-permute-start.8
  398.3 13.4 %collective-permute-start.4 = (bf16[2,2,256,1024]{3,2,1,0:T(8,128)(2,1)}, bf16[2,2,256,1024]{3,2,1,0:T(8,128)(2,1)}, u32[]{:S(2)}, u32[]{:S(2)}) collective-permute-start(bf16[2,2,256,1024]{3,2,1,0:T(8,128)(2,1)} %dynamic-slice_bitcast_fusion.1), channel_id=1, source_target_pairs={{0,1},{1,0},{2,3},{3,2},{4,5},{5,4},{6,7},{7,6},{8,9},{9,8},{10,11... | collective-permute-start | bytes 6291464 | tf_op jit(solution)/shard_map/ppermute | solution.py:474
  400.2 4.7 collective-permute-start.12
  402.8 21.0 %collective-permute-start.9 = (bf16[2,128,1024]{2,1,0:T(8,128)(2,1)S(1)}, bf16[2,128,1024]{2,1,0:T(8,128)(2,1)S(1)}, u32[]{:S(2)}, u32[]{:S(2)}) collective-permute-start(bf16[2,128,1024]{2,1,0:T(8,128)(2,1)S(1)} %dynamic-slice_bitcast_fusion.6), channel_id=1, source_target_pairs={{0,2},{2,0},{1,3},{3,1},{4,6},{6,4},{5,7},{7,5},{8,10},{10,8},{9,1... | collective-permute-start | bytes 1572872 | tf_op jit(solution)/shard_map/ppermute | solution.py:476
  409.5 53.9 %collective-permute-start.1 = (bf16[2,256,1024]{2,1,0:T(8,128)(2,1)S(1)}, bf16[2,256,1024]{2,1,0:T(8,128)(2,1)S(1)}, u32[]{:S(2)}, u32[]{:S(2)}) collective-permute-start(bf16[2,256,1024]{2,1,0:T(8,128)(2,1)S(1)} %dynamic-slice_bitcast_fusion.4), channel_id=1, source_target_pairs={{0,2},{2,0},{1,3},{3,1},{4,6},{6,4},{5,7},{7,5},{8,10},{10,8},{9,1... | collective-permute-start | bytes 3145736 | tf_op jit(solution)/shard_map/ppermute | solution.py:476
  409.9 53.0 %collective-permute-start.13 = (bf16[2,128,1024]{2,1,0:T(8,128)(2,1)S(1)}, bf16[2,128,1024]{2,1,0:T(8,128)(2,1)S(1)}, u32[]{:S(2)}, u32[]{:S(2)}) collective-permute-start(bf16[2,128,1024]{2,1,0:T(8,128)(2,1)S(1)} %dynamic-slice_bitcast_fusion.5), channel_id=1, source_target_pairs={{0,2},{2,0},{1,3},{3,1},{4,6},{6,4},{5,7},{7,5},{8,10},{10,8},{9,1... | collective-permute-start | bytes 1572872 | tf_op jit(solution)/shard_map/ppermute | solution.py:476
  414.3 82.6 %collective-permute-start.5 = (bf16[2,256,1024]{2,1,0:T(8,128)(2,1)S(1)}, bf16[2,256,1024]{2,1,0:T(8,128)(2,1)S(1)}, u32[]{:S(2)}, u32[]{:S(2)}) collective-permute-start(bf16[2,256,1024]{2,1,0:T(8,128)(2,1)S(1)} %dynamic-slice_bitcast_fusion.3), channel_id=1, source_target_pairs={{0,2},{2,0},{1,3},{3,1},{4,6},{6,4},{5,7},{7,5},{8,10},{10,8},{9,1... | collective-permute-start | bytes 3145736 | tf_op jit(solution)/shard_map/ppermute | solution.py:476
  424.0 72.8 %collective-permute-start.10 = (bf16[2,128,1024]{2,1,0:T(8,128)(2,1)S(1)}, bf16[2,128,1024]{2,1,0:T(8,128)(2,1)S(1)}, u32[]{:S(2)}, u32[]{:S(2)}) collective-permute-start(bf16[2,128,1024]{2,1,0:T(8,128)(2,1)S(1)} %fusion.66), channel_id=1, source_target_pairs={{0,2},{2,0},{1,3},{3,1},{4,6},{6,4},{5,7},{7,5},{8,10},{10,8},{9,1... | collective-permute-start | bytes 1572872 | tf_op jit(solution)/shard_map/ppermute | solution.py:478
  463.1 45.0 %collective-permute-start.14 = (bf16[2,128,1024]{2,1,0:T(8,128)(2,1)S(1)}, bf16[2,128,1024]{2,1,0:T(8,128)(2,1)S(1)}, u32[]{:S(2)}, u32[]{:S(2)}) collective-permute-start(bf16[2,128,1024]{2,1,0:T(8,128)(2,1)S(1)} %fusion.65), channel_id=1, source_target_pairs={{0,2},{2,0},{1,3},{3,1},{4,6},{6,4},{5,7},{7,5},{8,10},{10,8},{9,1... | collective-permute-start | bytes 1572872 | tf_op jit(solution)/shard_map/ppermute | solution.py:478
  463.8 67.2 %collective-permute-start.2 = (bf16[2,256,1024]{2,1,0:T(8,128)(2,1)S(1)}, bf16[2,256,1024]{2,1,0:T(8,128)(2,1)S(1)}, u32[]{:S(2)}, u32[]{:S(2)}) collective-permute-start(bf16[2,256,1024]{2,1,0:T(8,128)(2,1)S(1)} %fusion.53), channel_id=1, source_target_pairs={{0,2},{2,0},{1,3},{3,1},{4,6},{6,4},{5,7},{7,5},{8,10},{10,8},{9,1... | collective-permute-start | bytes 3145736 | tf_op jit(solution)/shard_map/ppermute | solution.py:478
  497.3 55.5 %collective-permute-start.6 = (bf16[2,256,1024]{2,1,0:T(8,128)(2,1)S(1)}, bf16[2,256,1024]{2,1,0:T(8,128)(2,1)S(1)}, u32[]{:S(2)}, u32[]{:S(2)}) collective-permute-start(bf16[2,256,1024]{2,1,0:T(8,128)(2,1)S(1)} %fusion.52), channel_id=1, source_target_pairs={{0,2},{2,0},{1,3},{3,1},{4,6},{6,4},{5,7},{7,5},{8,10},{10,8},{9,1... | collective-permute-start | bytes 3145736 | tf_op jit(solution)/shard_map/ppermute | solution.py:478
  497.8 56.6 %collective-permute-start.11 = (bf16[2,2,128,1024]{3,2,0,1:T(8,128)(2,1)S(1)}, bf16[2,2,128,1024]{3,2,0,1:T(8,128)(2,1)S(1)}, u32[]{:S(2)}, u32[]{:S(2)}) collective-permute-start(bf16[2,2,128,1024]{3,2,0,1:T(8,128)(2,1)S(1)} %pad_maximum_fusion.8), channel_id=1, source_target_pairs={{0,1},{1,0},{2,3},{3,2},{4,5},{5,4},{6,7},{7,6},{8,9},{9,8},{10,11... | collective-permute-start | bytes 3145736 | tf_op jit(solution)/shard_map/ppermute | solution.py:482
  508.3 46.7 %collective-permute-start.15 = (bf16[2,2,128,1024]{3,2,0,1:T(8,128)(2,1)S(1)}, bf16[2,2,128,1024]{3,2,0,1:T(8,128)(2,1)S(1)}, u32[]{:S(2)}, u32[]{:S(2)}) collective-permute-start(bf16[2,2,128,1024]{3,2,0,1:T(8,128)(2,1)S(1)} %pad_maximum_fusion.9), channel_id=1, source_target_pairs={{0,1},{1,0},{2,3},{3,2},{4,5},{5,4},{6,7},{7,6},{8,9},{9,8},{10,11... | collective-permute-start | bytes 3145736 | tf_op jit(solution)/shard_map/ppermute | solution.py:482
  533.1 107.8 %collective-permute-start.3 = (bf16[2,2,256,1024]{3,2,0,1:T(8,128)(2,1)}, bf16[2,2,256,1024]{3,2,0,1:T(8,128)(2,1)}, u32[]{:S(2)}, u32[]{:S(2)}) collective-permute-start(bf16[2,2,256,1024]{3,2,0,1:T(8,128)(2,1)} %pad_maximum_fusion.2), channel_id=1, source_target_pairs={{0,1},{1,0},{2,3},{3,2},{4,5},{5,4},{6,7},{7,6},{8,9},{9,8},{10,11... | collective-permute-start | bytes 6291464 | tf_op jit(solution)/shard_map/ppermute | solution.py:482
  554.4 91.7 %collective-permute-start.7 = (bf16[2,2,256,1024]{3,2,0,1:T(8,128)(2,1)}, bf16[2,2,256,1024]{3,2,0,1:T(8,128)(2,1)}, u32[]{:S(2)}, u32[]{:S(2)}) collective-permute-start(bf16[2,2,256,1024]{3,2,0,1:T(8,128)(2,1)} %pad_maximum_fusion.3), channel_id=1, source_target_pairs={{0,1},{1,0},{2,3},{3,2},{4,5},{5,4},{6,7},{7,6},{8,9},{9,8},{10,11... | collective-permute-start | bytes 6291464 | tf_op jit(solution)/shard_map/ppermute | solution.py:482
  (49 other events, 252.3 us)
Sparse Core Ops, SparseCore 0:
  12.2 25.2 all-gather.5
  63.6 31.4 reduce-scatter.3
  326.4 20.6 all-gather.9
  389.0 46.0 reduce-scatter.7
  438.5 89.0 reduce-scatter.5
Sparse Core Ops, SparseCore 1:
  66.3 100.0 all-gather.7
  382.6 152.2 all-reduce.5
  539.4 92.3 all-reduce.7

commit v2 on v1

--- a/solution.py
+++ b/solution.py
@@ -209,73 +209,400 @@
         compiler_params=pltpu.CompilerParams(collective_id=cid, has_side_effects=True),
     )(block)
 
-def ring_scatter(parts, cid):
-    count, rows, cols = parts.shape
-    lane = rows // 2
-    part = lane // 2
-
-    def kernel(p_ref, o_ref, held, send_sem, recv_sem):
-        me = lax.axis_index("wide")
-        place = ring_place(me, count)
-        at = lambda shift: ring_index((place + shift + 2 * count) % count, count)
-        peers = (at(1), at(-1))
-        ring_greet(*peers)
-
-        def copy(way, step, k):
-            sign = 1 if way == 0 else -1
-            span = pl.ds(k * part, part)
-            src = (
-                p_ref.at[at(-sign), pl.ds(way * lane + k * part, part)]
-                if step == 0
-                else held.at[way, step - 1, span]
-            )
-            return pltpu.make_async_remote_copy(
-                src_ref=src,
-                dst_ref=held.at[way, step, span],
-                send_sem=send_sem.at[way, step, k],
-                recv_sem=recv_sem.at[way, step, k],
-                device_id={"wide": peers[way]},
-                device_id_type=MESH,
-            )
-
-        for step in range(count - 1):
-            for k in range(2):
-                for way in range(2):
-                    sign = 1 if way == 0 else -1
-                    if step > 0:
-                        copy(way, step - 1, k).wait_recv()
-                        span = pl.ds(k * part, part)
-                        mine = p_ref[at(-sign * (1 + step)), pl.ds(way * lane + k * part, part)]
-                        held[way, step - 1, span] = (
-                            held[way, step - 1, span].astype(F32) + mine.astype(F32)
-                        ).astype(held.dtype)
-                    copy(way, step, k).start()
+
+def add_low(one, two):
+    return (one.astype(F32) + two.astype(F32)).astype(BF)
+
+class Ring:
+    def __init__(self, count):
+        self.count = count
+        self.me = lax.axis_index("wide")
+        self.place = ring_place(self.me, count)
+        self.peers = (self.at(1), self.at(-1))
+
+    def at(self, shift):
+        return ring_index((self.place + shift + 2 * self.count) % self.count, self.count)
+
+def greet(wide_peers, narrow_peers):
+    barrier = pltpu.get_barrier_semaphore()
+    for peer in wide_peers:
+        pl.semaphore_signal(barrier, inc=1, device_id={"wide": peer}, device_id_type=MESH)
+    for peer in narrow_peers:
+        pl.semaphore_signal(barrier, inc=1, device_id={"narrow": peer}, device_id_type=MESH)
+    pl.semaphore_wait(barrier, len(wide_peers) + len(narrow_peers))
+
+def remote(source, target, send, recv, **device):
+    return pltpu.make_async_remote_copy(
+        src_ref=source, dst_ref=target, send_sem=send, recv_sem=recv,
+        device_id=device, device_id_type=MESH,
+    )
+
+def cuts(rows):
+    first = (rows // 2 + 15) // 16 * 16
+    return ((0, first), (first, rows - first))
+
+def scatter_steps(ring, p_ref, held, send_sem, recv_sem, finish):
+    count = ring.count
+    lane = p_ref.shape[1] // 2
+
+    def copy(way, step, k):
+        sign = 1 if way == 0 else -1
+        start, size = cuts(lane)[k]
+        src = (
+            p_ref.at[ring.at(-sign), pl.ds(way * lane + start, size)]
+            if step == 0
+            else held.at[way, step - 1, pl.ds(start, size)]
+        )
+        return remote(
+            src, held.at[way, step, pl.ds(start, size)],
+            send_sem.at[way, step, k], recv_sem.at[way, step, k], wide=ring.peers[way],
+        )
+
+    for step in range(count - 1):
         for k in range(2):
             for way in range(2):
-                copy(way, count - 2, k).wait_recv()
-                rows_here = pl.ds(way * lane + k * part, part)
-                o_ref[rows_here] = held[way, count - 2, pl.ds(k * part, part)].astype(F32) + p_ref[
-                    me, rows_here
-                ].astype(F32)
-        for step in range(count - 1):
-            for k in range(2):
-                for way in range(2):
-                    copy(way, step, k).wait_send()
-
+                sign = 1 if way == 0 else -1
+                start, size = cuts(lane)[k]
+                if step > 0:
+                    copy(way, step - 1, k).wait_recv()
+                    span = pl.ds(start, size)
+                    mine = p_ref[ring.at(-sign * (1 + step)), pl.ds(way * lane + start, size)]
+                    held[way, step - 1, span] = add_low(held[way, step - 1, span], mine)
+                copy(way, step, k).start()
+        yield
+    for k in range(2):
+        for way in range(2):
+            start, size = cuts(lane)[k]
+            copy(way, count - 2, k).wait_recv()
+            row = way * lane + start
+            finish(
+                row, size,
+                held[way, count - 2, pl.ds(start, size)].astype(F32)
+                + p_ref[ring.me, pl.ds(row, size)].astype(F32),
+            )
+    for step in range(count - 1):
+        for k in range(2):
+            for way in range(2):
+                copy(way, step, k).wait_send()
+    yield
+
+def gather_steps(ring, o_ref, send_sem, recv_sem):
+    count = ring.count
+    hops = count // 2
+    rows = o_ref.shape[1]
+    live = lambda way, hop, k: hop < hops - 1 or k == way
+
+    def copy(way, hop, k, shift):
+        sign = 1 if way == 0 else -1
+        start, size = cuts(rows)[k]
+        block = o_ref.at[ring.at(-sign * (hop + shift)), pl.ds(start, size)]
+        return remote(
+            block, block, send_sem.at[way, hop, k], recv_sem.at[way, hop, k], wide=ring.peers[way]
+        )
+
+    for hop in range(hops):
+        for k in range(2):
+            for way in range(2):
+                if live(way, hop, k):
+                    if hop > 0:
+                        copy(way, hop - 1, k, 1).wait_recv()
+                    copy(way, hop, k, 0).start()
+        yield
+    for hop in range(hops):
+        for k in range(2):
+            for way in range(2):
+                if live(way, hop, k) and not (hop + 1 < hops and live(way, hop + 1, k)):
+                    copy(way, hop, k, 1).wait_recv()
+    for hop in range(hops):
+        for k in range(2):
+            for way in range(2):
+                if live(way, hop, k):
+                    copy(way, hop, k, 0).wait_send()
+    yield
+
+def scatter_scratch(count, rows, cols):
+    return [
+        pltpu.VMEM((2, count - 1, rows // 2, cols), BF),
+        pltpu.SemaphoreType.DMA((2, count - 1, 2)),
+        pltpu.SemaphoreType.DMA((2, count - 1, 2)),
+    ]
+
+def gather_scratch(count):
+    return [pltpu.SemaphoreType.DMA((2, count // 2, 2)), pltpu.SemaphoreType.DMA((2, count // 2, 2))]
+
+def run(*makers):
+    live = list(makers)
+    while live:
+        for one in list(live):
+            if next(one, "end") == "end":
+                live.remove(one)
+
+def block_add(out, one, two, rows):
+    def step(i, carry):
+        span = pl.ds(pl.multiple_of(i * 128, 128), 128)
+        out[span] = add_low(one[span], two[span])
+        return carry
+    lax.fori_loop(0, rows // 128, step, 0)
+
+def home_kernel(back, picks, expert_part, up_grads, down_grads, cid):
+    count, rows, cols = back.shape
+    paired = len(up_grads) > 0
+    pairs = len(up_grads)
+    each = up_grads[0].shape[0] if paired else 0
+    experts = pairs * each
+    quarter_up = up_grads[0].shape[1] // 4 if paired else 0
+    quarter_down = down_grads[0].shape[1] // 4 if paired else 0
+    quarter = quarter_up + quarter_down
+
+    def kernel(*refs):
+        refs = list(refs)
+        take = lambda number: [refs.pop(0) for _ in range(number)]
+        b_ref, p_ref, c_ref = take(3)
+        up_refs, down_refs = take(pairs), take(pairs)
+        ob_ref, op_ref, oc_ref = take(3)
+        if paired:
+            (own_ref,) = take(1)
+        b_scr, c_scr = take(3), take(3)
+        p_send, p_recv, p_own = take(3)
+        if paired:
+            got_a, mine, got_b, a_send, a_recv, l_sem, x_send, x_recv = take(8)
+        ring = Ring(count)
+        here = lax.axis_index("narrow")
+        chip, core = here // 2, here % 2
+        others = [(ring.me + shift) % count for shift in range(1, count)]
+        core_peer = 2 * chip + 1 - core
+        chip_peer = 2 * (1 - chip) + core
+        greet(others, [core_peer, chip_peer] if paired else [])
+
+        def piece_refs(expert, owner):
+            up, down = up_refs[expert // each], down_refs[expert // each]
+            return (
+                (up.at[expert % each, pl.ds(owner * quarter_up, quarter_up)], 0, quarter_up),
+                (down.at[expert % each, pl.ds(owner * quarter_down, quarter_down)], quarter_up, quarter_down),
+            )
+
+        def to_core(e):
+            return [
+                remote(src, got_a.at[e, x, pl.ds(start, size)], a_send.at[e, x, k], a_recv.at[e, x, k], narrow=core_peer)
+                for x in range(2)
+                for k, (src, start, size) in enumerate(piece_refs(e, 2 * x + 1 - core))
+            ]
+
+        def load(e):
+            return [
+                pltpu.make_async_copy(src, mine.at[e, x, pl.ds(start, size)], l_sem.at[e, x, k])
+                for x in range(2)
+                for k, (src, start, size) in enumerate(piece_refs(e, 2 * x + core))
+            ]
+
+        def to_chip(e):
+            return remote(mine.at[e, 1 - chip], got_b.at[e], x_send.at[e], x_recv.at[e], narrow=chip_peer)
+
+        def expert_first(e):
+            for c in to_core(e):
+                c.wait_recv()
+            for c in load(e):
+                c.wait()
+            block_add(mine.at[e, 1 - chip], mine.at[e, 1 - chip], got_a.at[e, 1 - chip], quarter)
+            to_chip(e).start()
+            block_add(mine.at[e, chip], mine.at[e, chip], got_a.at[e, chip], quarter)
+
+        def expert_last(e):
+            to_chip(e).wait_recv()
+            block_add(own_ref.at[e], mine.at[e, chip], got_b.at[e], quarter)
+
+        pick_copy = lambda k, target: remote(
+            p_ref.at[target], op_ref.at[ring.me], p_send.at[k], p_recv.at[k], wide=target
+        )
+        for e in range(experts):
+            for c in to_core(e):
+                c.start()
+            for c in load(e):
+                c.start()
+        own_pick = pltpu.make_async_copy(p_ref.at[ring.me], op_ref.at[ring.me], p_own)
+        own_pick.start()
+        for k, target in enumerate(others):
+            pick_copy(k, target).start()
+
+        def put(o_ref):
+            def finish(row, size, got):
+                o_ref[pl.ds(row, size)] = got.astype(o_ref.dtype)
+            return finish
+
+        b_steps = scatter_steps(ring, b_ref, *b_scr, put(ob_ref))
+        c_steps = scatter_steps(ring, c_ref, *c_scr, put(oc_ref))
+        queue = [(expert_first, e) for e in range(experts)]
+        later = [(expert_last, e) for e in range(experts)]
+        number = 0
+        for steps in (b_steps, c_steps):
+            for _ in steps:
+                number += 1
+                if queue:
+                    job, e = queue.pop(0)
+                    job(e)
+                elif later and number % 3 == 0:
+                    job, e = later.pop(0)
+                    job(e)
+        for job, e in queue + later:
+            job(e)
+        for e in range(experts):
+            for c in to_core(e):
+                c.wait_send()
+            to_chip(e).wait_send()
+        for k, target in enumerate(others):
+            sender = (ring.me - (k + 1) + count) % count
+            remote(
+                p_ref.at[sender], op_ref.at[sender], p_send.at[k], p_recv.at[k], wide=target
+            ).wait_recv()
+            pick_copy(k, target).wait_send()
+        own_pick.wait()
+
+    vmem = pl.BlockSpec(memory_space=pltpu.VMEM)
+    far = pl.BlockSpec(memory_space=pl.ANY)
+    out_shape = [
+        jax.ShapeDtypeStruct((rows, cols), F32),
+        jax.ShapeDtypeStruct(picks.shape, F32),
+        jax.ShapeDtypeStruct((rows, cols), F32),
+    ]
+    scratch = scatter_scratch(count, rows, cols) + scatter_scratch(count, rows, cols) + [
+        pltpu.SemaphoreType.DMA((count - 1,)),
+        pltpu.SemaphoreType.DMA((count - 1,)),
+        pltpu.SemaphoreType.DMA,
+    ]
+    if paired:
+        out_shape.append(jax.ShapeDtypeStruct((experts, quarter, cols), BF))
+        scratch += [
+            pltpu.VMEM((experts, 2, quarter, cols), BF),
+            pltpu.VMEM((experts, 2, quarter, cols), BF),
+            pltpu.VMEM((experts, quarter, cols), BF),
+            pltpu.SemaphoreType.DMA((experts, 2, 2)),
+            pltpu.SemaphoreType.DMA((experts, 2, 2)),
+            pltpu.SemaphoreType.DMA((experts, 2, 2)),
+            pltpu.SemaphoreType.DMA((experts,)),
+            pltpu.SemaphoreType.DMA((experts,)),
+        ]
     return pl.pallas_call(
         kernel,
-        out_shape=jax.ShapeDtypeStruct((rows, cols), F32),
-        in_specs=[pl.BlockSpec(memory_space=pltpu.VMEM)],
-        out_specs=pl.BlockSpec(memory_space=pltpu.VMEM),
-        scratch_shapes=[
-            pltpu.VMEM((2, count - 1, lane, cols), parts.dtype),
-            pltpu.SemaphoreType.DMA((2, count - 1, 2)),
-            pltpu.SemaphoreType.DMA((2, count - 1, 2)),
-        ],
+        out_shape=out_shape,
+        in_specs=[vmem] * 3 + [far] * (2 * pairs),
+        out_specs=[vmem] * len(out_shape),
+        scratch_shapes=scratch,
+        compiler_params=pltpu.CompilerParams(
+            collective_id=cid, has_side_effects=True, vmem_limit_bytes=56 * 2**20
+        ),
+    )(back, picks, expert_part, *up_grads, *down_grads)
+
+def last_kernel(packed, own, shapes, cid):
+    count, rows, cols = packed.shape
+    paired = own is not None
+    if paired:
+        experts, quarter, width = own.shape
+        up_shape, down_shape = shapes
+        quarter_up, quarter_down = up_shape[1] // 4, down_shape[1] // 4
+
+    def kernel(*refs):
+        refs = list(refs)
+        take = lambda number: [refs.pop(0) for _ in range(number)]
+        (p_ref,) = take(1)
+        if paired:
+            (own_ref,) = take(1)
+        (o_ref,) = take(1)
+        if paired:
+            up_ref, down_ref = take(2)
+        s_scr, g_scr = take(3), take(2)
+        if paired:
+            c_send, c_recv, x_send, x_recv, f_send, f_recv, l_sem = take(7)
+        ring = Ring(count)
+        here = lax.axis_index("narrow")
+        chip, core = here // 2, here % 2
+        core_peer = 2 * chip + 1 - core
+        chip_peer = 2 * (1 - chip) + core
+        greet(list(ring.peers), [core_peer, chip_peer] if paired else [])
+
+        def places(e, owner):
+            return (
+                (own_ref.at[e, pl.ds(0, quarter_up)], up_ref.at[e, pl.ds(owner * quarter_up, quarter_up)]),
+                (own_ref.at[e, pl.ds(quarter_up, quarter_down)], down_ref.at[e, pl.ds(owner * quarter_down, quarter_down)]),
+            )
+
+        def send(e, sems, peer):
+            return [
+                remote(src, dst, sems[0].at[e, k], sems[1].at[e, k], narrow=peer)
+                for k, (src, dst) in enumerate(places(e, here))
+            ]
+
+        def forward(e, owner, sems, peer):
+            return [
+                remote(dst, dst, sems[0].at[e, k], sems[1].at[e, k], narrow=peer)
+                for k, (src, dst) in enumerate(places(e, owner))
+            ]
+
+        core_sems, chip_sems, far_sems = ((c_send, c_recv), (x_send, x_recv), (f_send, f_recv)) if paired else (None,) * 3
+
+        def own_copy(e):
+            return [
+                pltpu.make_async_copy(src, dst, l_sem.at[e, k])
+                for k, (src, dst) in enumerate(places(e, here))
+            ]
+
+        def pass_on(e):
+            for c in forward(e, chip_peer, chip_sems, chip_peer):
+                c.wait_recv()
+            for c in forward(e, chip_peer, far_sems, core_peer):
+                c.start()
+
+        experts_here = experts if paired else 0
+        for e in range(experts_here):
+            for c in send(e, chip_sems, chip_peer):
+                c.start()
+        for e in range(experts_here):
+            for c in send(e, core_sems, core_peer) + own_copy(e):
+                c.start()
+
+        def finish(row, size, got):
+            o_ref[ring.me, pl.ds(row, size)] = got.astype(BF)
+
+        waiting = list(range(experts_here))
+        number = 0
+        for steps in (scatter_steps(ring, p_ref, *s_scr, finish), gather_steps(ring, o_ref, *g_scr)):
+            for _ in steps:
+                number += 1
+                if waiting and number % 4 == 0:
+                    pass_on(waiting.pop(0))
+        for e in waiting:
+            pass_on(e)
+        for e in range(experts_here):
+            for c in own_copy(e):
+                c.wait()
+            for c in send(e, chip_sems, chip_peer) + send(e, core_sems, core_peer):
+                c.wait_send()
+            for c in forward(e, core_peer, core_sems, core_peer):
+                c.wait_recv()
+            far_owner = 2 * (1 - chip) + 1 - core
+            for c in forward(e, chip_peer, far_sems, core_peer):
+                c.wait_send()
+            for c in forward(e, far_owner, far_sems, core_peer):
+                c.wait_recv()
+
+    vmem = pl.BlockSpec(memory_space=pltpu.VMEM)
+    far = pl.BlockSpec(memory_space=pl.ANY)
+    out_shape = [jax.ShapeDtypeStruct(packed.shape, BF)]
+    operands = [packed]
+    scratch = scatter_scratch(count, rows, cols) + gather_scratch(count)
+    if paired:
+        out_shape += [jax.ShapeDtypeStruct(s, BF) for s in shapes]
+        operands.append(own)
+        scratch += [pltpu.SemaphoreType.DMA((experts, 2))] * 7
+    return pl.pallas_call(
+        kernel,
+        out_shape=out_shape,
+        in_specs=[vmem] + [far] * (len(operands) - 1),
+        out_specs=[vmem] + [far] * (len(out_shape) - 1),
+        scratch_shapes=scratch,
         compiler_params=pltpu.CompilerParams(
             collective_id=cid, has_side_effects=True, vmem_limit_bytes=40 * 2**20
         ),
-    )(parts)
+    )(*operands)
 
 
 TILE = 256
@@ -463,34 +790,6 @@
     )(offsets, *operands)
 
 
-def pair_sum(parts):
-    here = lax.axis_index("narrow")
-    chip, core = here // 2, here % 2
-    to_core = [(0, 1), (1, 0), (2, 3), (3, 2)]
-    to_chip = [(0, 2), (2, 0), (1, 3), (3, 1)]
-    pick = lambda array, index, axis: lax.dynamic_index_in_dim(array, index, axis, keepdims=False)
-    add = lambda one, two: (one.astype(F32) + two.astype(F32)).astype(BF)
-    cubes = [p.reshape(p.shape[0], 2, 2, p.shape[1] // 4, p.shape[2]) for p in parts]
-    got = [lax.ppermute(pick(c, 1 - core, 2), "narrow", to_core) for c in cubes]
-    half = [add(pick(c, core, 2), g) for c, g in zip(cubes, got)]
-    got = [lax.ppermute(pick(h, 1 - chip, 1), "narrow", to_chip) for h in half]
-    own = [add(pick(h, chip, 1), g) for h, g in zip(half, got)]
-    other = [lax.ppermute(o, "narrow", to_chip) for o in own]
-    done = []
-    for o, t in zip(own, other):
-        mine = jnp.stack([jnp.where(chip == 0, o, t), jnp.where(chip == 0, t, o)], axis=1)
-        theirs = lax.ppermute(mine, "narrow", to_core)
-        both = jnp.stack([jnp.where(core == 0, mine, theirs), jnp.where(core == 0, theirs, mine)], axis=2)
-        done.append(both.reshape(o.shape[0], 4 * o.shape[1], o.shape[2]).astype(F32))
-    return done
-
-
-def narrow_sum(parts):
-    if lax.axis_size("narrow") == 4:
-        return pair_sum(parts)
-    return [lax.psum(p, "narrow").astype(F32) for p in parts]
-
-
 def local(
     hidden,
     lengths,
@@ -609,16 +908,14 @@
         earlier = (expert_part, back_part)
         pick_parts.append(pick_part)
         weight_parts.append((up_part, down_part))
-    entry_home = ring_scatter(back_part, 2)
-    pick_home = lax.all_to_all(
-        jnp.concatenate(pick_parts, axis=0), "wide", split_axis=1, concat_axis=0, tiled=True
-    ).reshape(expert_total, rows_here)
-    summed = [narrow_sum(p) for p in weight_parts]
-    gate_up_grad = jnp.concatenate([s[0] for s in summed], axis=0)
-    down_grad = jnp.concatenate([s[1] for s in summed], axis=0)
-
-    expert_part, entry_home = lax.optimization_barrier((expert_part, entry_home))
-    expert_sum = lax.psum_scatter(expert_part, "wide", scatter_dimension=0, tiled=False).astype(F32)
+    picks_out = jnp.concatenate(pick_parts, axis=0).transpose(1, 0, 2)
+    paired = lax.axis_size("narrow") == 4
+    ups = [p[0] for p in weight_parts]
+    downs = [p[1] for p in weight_parts]
+    entry_home, pick_home, expert_sum, *own = home_kernel(
+        back_part, picks_out, expert_part, ups if paired else [], downs if paired else [], 2
+    )
+    pick_home = pick_home.reshape(expert_total, rows_here)
     output_rows = (valid * (mixed + expert_sum)).astype(jnp.bfloat16)
     grad_rows_here = cotangent[0].astype(jnp.float32) * valid
 
@@ -676,15 +973,33 @@
     source_from_norm, gain_one_grad = norm_backward(source, scale_one, attn_gain, normed_grad)
     grad_input = (mixed_grad + source_from_norm).astype(jnp.bfloat16)
     gain_one_grad = jnp.sum(qkv_weight_grad * w_qkv.astype(F32), axis=1) / attn_gain
-    small = jnp.concatenate([router_grad, gain_one_grad[:, None], gain_two_grad[:, None]], axis=1)
-    small = lax.psum(small, ("wide", "narrow"))
-    router_grad = small[:, :expert_total]
-    gain_one_grad = small[:, expert_total]
-    gain_two_grad = small[:, expert_total + 1]
-    qkv_weight_grad, out_grad = (
-        lax.psum(qkv_weight_grad.astype(jnp.bfloat16), "wide").astype(jnp.float32),
-        lax.psum(out_grad.astype(jnp.bfloat16), "wide").astype(jnp.float32),
-    )
+    small = jnp.concatenate(
+        [router_grad.T, gain_one_grad[None], gain_two_grad[None], jnp.zeros((14, width), F32)], axis=0
+    )
+    small = lax.psum(small.astype(BF), "narrow").astype(F32)
+    lanes = query_cols + 2 * key_cols
+    rows_of = lambda array: [array[:, i : i + lanes] for i in range(0, width, lanes)]
+    flat = jnp.concatenate([qkv_weight_grad, *rows_of(out_grad), *rows_of(small)], axis=0).astype(BF)
+    block = -(-flat.shape[0] // (32 * wide)) * 32
+    packed = jnp.pad(flat, ((0, block * wide - flat.shape[0]), (0, 0))).reshape(wide, block, lanes)
+    summed, *expert_grads = last_kernel(
+        packed, own[0] if paired else None, (w_gate_up.shape, w_down.shape), 3
+    )
+    if paired:
+        gate_up_grad, down_grad = expert_grads[0].astype(F32), expert_grads[1].astype(F32)
+    else:
+        gate_up_grad = lax.psum(jnp.concatenate(ups, axis=0), "narrow").astype(F32)
+        down_grad = lax.psum(jnp.concatenate(downs, axis=0), "narrow").astype(F32)
+    summed = summed.reshape(wide * block, lanes).astype(F32)
+    qkv_weight_grad = summed[:width]
+    blocks_of = lambda start, rows: jnp.concatenate(
+        [summed[start + i * rows : start + (i + 1) * rows] for i in range(width // lanes)], axis=1
+    )
+    out_grad = blocks_of(width, query_cols)
+    small = blocks_of(width + query_cols * (width // lanes), small.shape[0])
+    router_grad = small[:expert_total].T
+    gain_one_grad = small[expert_total]
+    gain_two_grad = small[expert_total + 1]
     query_weight_grad = qkv_weight_grad[:, :query_cols]
     key_weight_grad = qkv_weight_grad[:, query_cols : query_cols + key_cols]
     value_weight_grad = qkv_weight_grad[:, query_cols + key_cols :]

time: 676 us -> 603 us (0.89)
  waiting for transfers between devices: 247 us -> 65.4 us
  Pallas kernels: 193 us -> 332 us
  starting transfers between devices: 20.5 us -> 0.25 us
  other arithmetic: 71.6 us -> 54.6 us
  matrix products: 47.4 us -> 61.6 us
  local copies, waits for them, and re-layouts: 45.2 us -> 32.4 us
    pallas_call x1 -> x2, Pallas kernels: 40.7 us -> 190 us  [the longest x1 107 us: home_kernel(): pl.pallas_call(kernel, out_shape=out_shape, in_specs=[vmem] * 3 + [far] *...]
    ppermute x16 -> x0, waiting for transfers between devices: 133 us -> none  [the longest x4 83.7 us: pair_sum(): other = [lax.ppermute(o, 'narrow', to_chip) for o in own]]
    psum x2 -> x1, waiting for transfers between devices: 69.4 us -> 25.1 us  [local(): small = lax.psum(small.astype(BF), 'narrow').astype(F32)]
    concatenate x4 -> x2, other arithmetic: 16.2 us -> 1.79 us  [the longest x1 1.06 us: local(): jnp.concatenate([summed[start + i * rows:start + (i + 1) * rows] for i in...]
    all_to_all x1 -> x0, starting transfers between devices: 12.7 us -> none  [local(): lax.all_to_all(jnp.concatenate(pick_parts, axis=0), 'wide', split_axis=1,...]
    pallas_call x2, Pallas kernels: 83.1 us -> 72.7 us  [expert_pair(): pl.pallas_call(kernel, grid_spec=pltpu.PrefetchScalarGridSpec(num_scalar_...]
    another operation x21 -> x6, other arithmetic: 10.2 us -> 0.47 us  [the longest x8 5.97 us: pair_sum(): jnp.stack([jnp.where(core == 0, mine, theirs), jnp.where(core == 0, their...]
    ppermute x16 -> x0, starting transfers between devices: 6.95 us -> none  [the longest x4 2.93 us: pair_sum(): got = [lax.ppermute(pick(h, 1 - chip, 1), 'narrow', to_chip) for h in half]]
  transfers between devices with their start and end apart: 25 -> 6, of which waited for: 10 -> 3; matrix products, arithmetic and copies ran while one was open for 13% -> 9% of each run, Pallas kernels for 16% -> 26%
where the time goes in v2:
time: 603 us; the launch traced here: 595 us
  Pallas kernels  332 us (55%)
  waiting for transfers between devices  65.4 us (11%)
  matrix products  61.6 us (10%)
  other arithmetic  54.6 us (9%)
  local copies, waits for them, and re-layouts  32.4 us (5%)
  blocking collectives  31.4 us (5%)
  between operations  17.2 us (3%)
    pallas_call x1, Pallas kernels, home_kernel(): pl.pallas_call(kernel, out_shape=out_shape, in_specs=[vmem] * 3 + [far] *...  107 us
    pallas_call x1, Pallas kernels, last_kernel(): pl.pallas_call(kernel, out_shape=out_shape, in_specs=[vmem] + [far] * (le...  83.9 us
    pallas_call x2, Pallas kernels, expert_pair(): pl.pallas_call(kernel, grid_spec=pltpu.PrefetchScalarGridSpec(num_scalar_...  72.7 us
    pallas_call x1, Pallas kernels, ring_gather(): pl.pallas_call(kernel, out_shape=jax.ShapeDtypeStruct((count, rows, cols)...  69 us
    all_gather x1, blocking collectives, local(): labels_all = lax.all_gather(labels, 'wide', axis=0)  31.4 us
    psum x1, waiting for transfers between devices, local(): small = lax.psum(small.astype(BF), 'narrow').astype(F32)  25.1 us
    all_gather x1, waiting for transfers between devices, local(): whole = lax.all_gather(normed_low, 'narrow', axis=0, tiled=True)  21 us
    all_gather x1, waiting for transfers between devices, local(): grad_whole = lax.all_gather(attn_grad_low, 'narrow', axis=0, tiled=True)  18.7 us
  transfers between devices with their start and end apart: 6, of which 3 were waited for; matrix products, arithmetic and copies ran while one was open for 9% of the time, Pallas kernels for 26%

profile of v2, /device:TPU:0, one launch (start us, length us, event | category | flops | bytes accessed | tf_op | source)
XLA Modules:
  0.0 595.2 jit_solution(10597669567737251065)
XLA Ops:
  16.4 21.0 %all-gather.6.cloned.1.call-done = bf16[1024,1024]{1,0:T(8,128)(2,1)} async-done(((bf16[256,1024]{1,0:T(8,128)(2,1)}), bf16[1024,1024]{1,0:T(8,128)(2,1)}) %all-gather.6.cloned.1.call-update) | async-done | bytes 2097168 | tf_op jit(solution)/shard_map/all_gather | solution.py:853
  37.4 2.9 fusion.98
  41.8 18.7 %while.30 = (s32[]{:T(128)}, bf16[2,2,2,512,64]{3,4,2,1,0:T(8,128)(2,1)S(1)}, f32[2,2,2,512]{3,2,1,0:T(2,128)S(1)}, s32[2]{0:T(128)S(1)}, s32[]{:T(128)}, /*inde...) while((s32[]{:T(128)}, ...), condition=%wide.region_4.5_spmd.clone.clone, body=%wide.region_1.4_spmd.clone.clone.sunk | while | flops 563215872 | bytes 28383356 | solution.py:79
  45.8 2.4 fusion.135
  48.2 3.0 fusion.136
  55.2 2.4 fusion.135
  57.6 3.0 fusion.136
  65.4 31.4 %all-gather.1 = s32[8,9,256]{2,1,0:T(8,128)S(1)} all-gather(s32[1,9,256]{2,1,0:T(8,128)S(1)} %pad_bitcast_fusion), channel_id=2, replica_groups=mesh['wide'=8,'narrow'=4] {'wide'}, dimensions={0}, use_global_device_ids=true | all-gather | bytes 82944 | tf_op jit(solution)/shard_map/all_gather | solution.py:833
  101.2 2.3 copy.82.s_ref
  109.2 69.0 %shard_map.212.e_ref = bf16[8,256,1024]{2,1,0:T(8,128)(2,1)} custom-call(bf16[256,1024]{1,0:T(8,128)(2,1)} %multiply_convert_fusion.2.x_ref), custom_call_target="tpu_custom_call" | custom-call | tf_op jit(solution)/shard_map/pallas_call | solution.py:199
  178.2 3.5 fusion.78
  183.0 32.0 %shard_map.213 = (bf16[8,256,1024]{2,1,0:T(8,128)(2,1)}, bf16[8,256,1024]{2,1,0:T(8,128)(2,1)}, f32[2,8,256]{2,1,0:T(8,128)}, bf16[2,1024,1024]{2,1,0:T(8,128)(2,1)}, bf16[2,512,1024]{2,1,0:T(8,128)(2,1)}) custom-call(s32[36]{0:T(128)} %reshape.281.off_ref, bf16[8,256,1024]{2,1,0:T(8,128)(2,1)} %shard_map.212.e_ref, ...), custom_call_target="tpu_custom_call" | custom-call | flops 19327352832 | bytes 41943040 | tf_op jit(solution)/shard_map/pallas_call | solution.py:753
  215.0 40.7 %shard_map.214 = (bf16[8,256,1024]{2,1,0:T(8,128)(2,1)}, bf16[8,256,1024]{2,1,0:T(8,128)(2,1)}, f32[2,8,256]{2,1,0:T(8,128)}, bf16[2,1024,1024]{2,1,0:T(8,128)(2,1)}, bf16[2,512,1024]{2,1,0:T(8,128)(2,1)}) custom-call(s32[36]{0:T(128)} %reshape.281.off_ref, bf16[8,256,1024]{2,1,0:T(8,128)(2,1)} %shard_map.212.e_ref, ...), custom_call_target="tpu_custom_call" | custom-call | flops 19327352832 | bytes 41943040 | tf_op jit(solution)/shard_map/pallas_call | solution.py:753
  257.1 106.5 %shard_map.215 = (f32[256,1024]{1,0:T(8,128)}, f32[8,4,256]{2,1,0:T(4,128)}, f32[256,1024]{1,0:T(8,128)}, bf16[4,384,1024]{2,1,0:T(8,128)(2,1)}) custom-call(bf16[8,256,1024]{2,1,0:T(8,128)(2,1)} %get-tuple-element.149.refs_0_, f32[8,4,256]{2,1,0:T(4,128)} %maximum_bitcast_fusion.2.refs_1_, bf16[8,256,1024]{2,1,0:T(8,128)(2,1)} %get-tuple-element.152.refs_2_, ...), custom_call_target="tpu_custom_call" | custom-call | tf_op jit(solution)/shard_map/pallas_call | solution.py:484
  371.8 18.7 %all-gather.10.cloned.1.call-done = bf16[1024,1024]{1,0:T(8,128)(2,1)} async-done(((bf16[256,1024]{1,0:T(8,128)(2,1)}), bf16[1024,1024]{1,0:T(8,128)(2,1)}) %all-gather.10.cloned.1.call-update) | async-done | bytes 2097168 | tf_op jit(solution)/shard_map/all_gather | solution.py:933
  390.5 2.3 convolution_convert_fusion.4
  393.6 44.7 %while.31 = (s32[]{:T(128)}, f32[2,1024,64]{1,2,0:T(8,128)S(1)}, f32[2,1024,64]{1,2,0:T(8,128)S(1)}, f32[2,2,2,512,64]{3,4,2,1,0:T(8,128)}, s32[2]{0:T(128)S(1)}...) while((s32[]{:T(128)}, f32[2,1024,64]{1,2,0:T(8,128)S(1)}, ...), condition=%wide.region_15.16_spmd.clone.clone, body=%wide.region_13.15_spmd.clone.clone.sunk | while | flops 1364983296 | bytes 118799088 | solution.py:122
  397.2 3.7 multiply_reduce_fusion.6
  401.8 2.5 copy-done.4
  408.5 3.1 fusion.147
  411.6 4.3 fusion.148
  419.5 3.7 multiply_reduce_fusion.6
  424.1 2.5 copy-done.4
  430.8 3.1 fusion.147
  433.9 4.3 fusion.148
  442.8 3.9 convolution_convert_fusion
  446.7 2.3 convolution_convert_fusion.3
  449.0 25.1 %all-reduce.5.cloned.1.call-done = bf16[48,1024]{1,0:T(8,128)(2,1)} async-done(((bf16[48,1024]{1,0:T(8,128)(2,1)}), bf16[48,1024]{1,0:T(8,128)(2,1)}) %all-reduce.5.cloned.1.call-update) | async-done | bytes 98320 | tf_op jit(solution)/shard_map/psum | solution.py:979
  477.8 83.9 %shard_map.216 = (bf16[8,224,512]{2,1,0:T(8,128)(2,1)S(1)}, bf16[4,1024,1024]{2,1,0:T(8,128)(2,1)}, bf16[4,512,1024]{2,1,0:T(8,128)(2,1)S(1)}) custom-call(bf16[8,224,512]{2,1,0:T(8,128)(2,1)S(1)} %bitcast.254, bf16[4,384,1024]{2,1,0:T(8,128)(2,1)S(1)} %copy-done.2), custom_call_target="tpu_custom_call" | custom-call | tf_op jit(solution)/shard_map/pallas_call | solution.py:596
  561.7 11.7 %convert_element_type.112 = f32[4,1024,1024]{2,1,0:T(8,128)} convert(bf16[4,1024,1024]{2,1,0:T(8,128)(2,1)} %get-tuple-element.166) | non-fusion elementwise | flops 4194304 | bytes 25165824 | tf_op jit(solution)/shard_map/convert_element_type | solution.py:989
  573.4 4.4 convert_element_type.113
  584.5 3.2 fusion.65
  (215 shorter events, 75.1 us)
Async XLA Ops:
  8.0 54.0 %copy-start = (bf16[256,1024]{1,0:T(8,128)(2,1)S(1)}, bf16[256,1024]{1,0:T(8,128)(2,1)}, u32[]{:S(2)}) copy-start(bf16[256,1024]{1,0:T(8,128)(2,1)} %param.25) | copy-start | bytes 1572868
  8.0 29.4 %all-gather.6.cloned.1.call-start = ((), (), s32[]{:S(2)}) async-start(), calls=%async_computation.2 | async-start | bytes 2621440 | tf_op jit(solution)/shard_map/all_gather | solution.py:853
  11.9 93.8 %reduce-scatter.3.cloned.1.call-start = ((), (), s32[]{:S(2)}) async-start(), calls=%async_computation.3 | async-start | bytes 2621440 | tf_op jit(solution)/shard_map/reduce_scatter | solution.py:883
  15.2 25.1 %copy-start.16 = (bf16[1024,512]{1,0:T(8,128)(2,1)}, bf16[1024,512]{1,0:T(8,128)(2,1)S(1)}, u32[]{:S(2)}) copy-start(bf16[1024,512]{1,0:T(8,128)(2,1)S(1)} %constant_dynamic-update-slice_fusion) | copy-start | bytes 3145732
  16.4 24.1 %copy-start.14 = (f32[1024,32]{0,1:T(8,128)}, f32[1024,32]{0,1:T(8,128)S(1)}, u32[]{:S(2)}) copy-start(f32[1024,32]{0,1:T(8,128)S(1)} %get-tuple-element.418) | copy-start | bytes 393220
  60.6 37.2 %copy-start.36 = (s32[2]{0:T(128)}, s32[2]{0:T(128)S(1)}, u32[]{:S(2)}) copy-start(s32[2]{0:T(128)S(1)} %get-tuple-element.639) | copy-start | bytes 28
  60.6 4.8 copy-start.34
  64.1 41.7 %copy-start.5 = (bf16[1,256,1024]{2,1,0:T(8,128)(2,1)S(1)}, bf16[1,256,1024]{2,1,0:T(8,128)(2,1)}, u32[]{:S(2)}) copy-start(bf16[1,256,1024]{2,1,0:T(8,128)(2,1)} %param.17) | copy-start | bytes 1572868
  64.1 43.0 %copy-start.25 = (f32[1024]{0:T(1024)S(1)}, f32[1024]{0:T(1024)}, u32[]{:S(2)}) copy-start(f32[1024]{0:T(1024)} %param.26) | copy-start | bytes 12292
  64.1 118.9 %all-gather.8.cloned.1.call-start = ((), (), s32[]{:S(2)}) async-start(), calls=%async_computation.4 | async-start | bytes 4718592 | tf_op jit(solution)/shard_map/all_gather | solution.py:824
  64.7 325.8 %all-gather.10.cloned.1.call-start = ((), (), s32[]{:S(2)}) async-start(), calls=%async_computation.5 | async-start | bytes 2621440 | tf_op jit(solution)/shard_map/all_gather | solution.py:933
  101.2 77.0 %copy-start.22 = (bf16[1024,32]{0,1:T(8,128)(2,1)S(1)}, bf16[1024,32]{0,1:T(8,128)(2,1)}, u32[]{:S(2)}) copy-start(bf16[1024,32]{0,1:T(8,128)(2,1)} %param.27) | copy-start | bytes 196612
  107.1 71.1 %copy-start.28 = (f32[256]{0:T(256)}, f32[256]{0:T(256)S(1)}, u32[]{:S(2)}) copy-start(f32[256]{0:T(256)S(1)} %add_rsqrt_fusion) | copy-start | bytes 3076
  215.0 41.4 %copy-start.30 = (f32[2,8,256]{2,1,0:T(8,128)S(1)}, f32[2,8,256]{2,1,0:T(8,128)}, u32[]{:S(2)}) copy-start(f32[2,8,256]{2,1,0:T(8,128)} %get-tuple-element.150) | copy-start | bytes 49156
  257.1 107.4 %copy-start.7 = (bf16[256,1024]{1,0:T(8,128)(2,1)S(1)}, bf16[256,1024]{1,0:T(8,128)(2,1)}, u32[]{:S(2)}) copy-start(bf16[256,1024]{1,0:T(8,128)(2,1)} %reduce-scatter.3.cloned.1.call-done) | copy-start | bytes 1572868
  257.1 110.6 %copy-start.11 = (bf16[1,256,1024]{2,1,0:T(8,128)(2,1)S(1)}, bf16[1,256,1024]{2,1,0:T(8,128)(2,1)}, u32[]{:S(2)}) copy-start(bf16[1,256,1024]{2,1,0:T(8,128)(2,1)} %param.20) | copy-start | bytes 1572868
  369.6 104.5 %all-reduce.5.cloned.1.call-start = ((), (), s32[]{:S(2)}) async-start(), calls=%async_computation.7 | async-start | bytes 196608 | tf_op jit(solution)/shard_map/psum | solution.py:979
  371.8 21.7 %copy-start.37 = (s32[2]{0:T(128)S(1)}, s32[2]{0:T(128)}, u32[]{:S(2)}) copy-start(s32[2]{0:T(128)} %copy-done.36) | copy-start | bytes 28
  393.5 46.2 %copy-start.15 = (f32[1024,32]{0,1:T(8,128)S(1)}, f32[1024,32]{0,1:T(8,128)}, u32[]{:S(2)}) copy-start(f32[1024,32]{0,1:T(8,128)} %copy-done.14) | copy-start | bytes 393220
  393.5 46.2 %copy-start.20 = (f32[1024,32]{0,1:T(8,128)S(1)}, f32[1024,32]{0,1:T(8,128)}, u32[]{:S(2)}) copy-start(f32[1024,32]{0,1:T(8,128)} %get-tuple-element.416) | copy-start | bytes 393220
  400.9 3.4 copy-start.4
  442.7 4.0 copy-start.19
  442.7 140.3 %reduce-scatter.5.cloned.1.call-start = ((), (), s32[]{:S(2)}) async-start(), calls=%async_computation.6 | async-start | bytes 2621440 | tf_op jit(solution)/shard_map/reduce_scatter | solution.py:965
  578.4 4.6 copy-start.6
  578.4 4.6 copy-start.32
  579.5 4.9 copy-start.8
  579.5 4.9 copy-start.10
  579.5 4.9 copy-start.12
  579.5 4.9 copy-start.26
  579.5 4.9 copy-start.29
  579.5 4.9 copy-start.33
  580.9 6.7 %copy-start.1 = (bf16[256,1024]{1,0:T(8,128)(2,1)S(1)}, bf16[256,1024]{1,0:T(8,128)(2,1)}, u32[]{:S(2)}) copy-start(bf16[256,1024]{1,0:T(8,128)(2,1)} %param.25) | copy-start | bytes 1572868
  (14 other events, 22.2 us)
Sparse Core Ops, SparseCore 0:
  12.1 25.2 all-gather.5
  64.2 31.4 reduce-scatter.2
  369.8 20.7 all-gather.9
  442.8 31.2 all-reduce.4
  476.5 43.5 reduce-scatter.4
Sparse Core Ops, SparseCore 1:
  67.0 98.4 all-gather.7
